TPU v7x, 128 devices: a whole 4x4x4 slice. The times are simulated.
128 devices in a mesh: gr: 8 (over x, core), gc: 8 (over y, z_lo), dr: 2 (over z_hi).
Axes of the slice: x: 4, y: 4, z: 4 (z_hi: 2, z_lo: 2; z = z_hi * 2 + z_lo), core: 2. Of those that a mesh axis runs over, the one named last changes fastest.
Arguments:
- draft_rows: bfloat16 [512, 14848], P('gr', ('gc', 'dr')), may hold values from -6 to 6
- tree_sizes: int32 [64], replicated, may hold values from 1 to 128, 512 in all
- draft_map: int32 [64], replicated, may hold values from 0 to 15
- row_order: int32 [512], replicated, may hold values from 0 to 511, each once
- up_weight: bfloat16 [14848, 53248], P(('gc', 'dr'), 'gr'), may hold values from -0.046875 to 0.046875
- down_weight: bfloat16 [53248, 14848], P('gr', ('gc', 'dr')), may hold values from -0.02734375 to 0.02734375
Outputs:
- verified: bfloat16 [512, 14848], P('gr', ('gc', 'dr'))
Inputs may be any that keep to these rules, and one draw needn't show every extreme that they name: `tree_sizes`: tree sizes sum to 512; some request has exactly 128. `row_order`: each position appears once.
All inputs are finite; a program needn't handle non-finite values.
Results may differ from a plain program's by a relative error of at most 0.005.
Values may be sent and summed in bfloat16 or wider, within the bound.
No kernel may reach another device: no remote copies, remote signals or barrier semaphores. Data moves between devices by JAX's collectives and lax.ppermute only.
A program may use at most 128 MiB of HBM per device.

v0:
```python
import jax
import jax.numpy as jnp
from jax import lax
from jax.sharding import PartitionSpec as P


def source_rows(tree_sizes, draft_map, row_order):
    ends = jnp.cumsum(tree_sizes)
    req_start = ends - tree_sizes
    reqs = jnp.arange(tree_sizes.shape[0], dtype=jnp.int32)
    before = (draft_map[None, :] < draft_map[:, None]) | (
        draft_map[None, :] == draft_map[:, None]
    ) & (reqs[None, :] < reqs[:, None])
    draft_start = jnp.sum(jnp.where(before, tree_sizes[None, :], 0), axis=1)
    owner = jnp.sum((row_order[:, None] >= ends[None, :]).astype(jnp.int32), axis=1)
    return draft_start[owner] + row_order - req_start[owner]


def on_device(draft_rows, tree_sizes, draft_map, row_order, up_weight, down_weight):
    gathered = lax.all_gather(draft_rows, "gr", axis=0, tiled=True)
    source = source_rows(tree_sizes, draft_map, row_order)
    candidates = gathered[source]
    partial_value = jnp.dot(candidates, up_weight, preferred_element_type=jnp.float32)
    pre = lax.psum(partial_value, ("gc", "dr"))
    hidden = jax.nn.gelu(pre, approximate=False).astype(jnp.bfloat16)
    result = lax.psum_scatter(
        jnp.dot(hidden, down_weight, preferred_element_type=jnp.float32),
        "gr",
        scatter_dimension=0,
        tiled=True,
    )
    return result.astype(jnp.bfloat16)


def solution(mesh):
    return jax.shard_map(
        on_device,
        mesh=mesh,
        in_specs=(
            P("gr", ("gc", "dr")),
            P(),
            P(),
            P(),
            P(("gc", "dr"), "gr"),
            P("gr", ("gc", "dr")),
        ),
        out_specs=P("gr", ("gc", "dr")),
        check_vma=False,
    )
```

profile of v0, /device:TPU:1, one launch (start us, length us, event | category | flops | bytes accessed | tf_op | source)
XLA Modules:
  0.0 399.5 jit_solution(4898266797789358890)
XLA Ops:
  6.5 0.9 select_reduce_fusion
  7.4 0.7 fusion.47
  8.1 0.7 fusion.44
  8.9 0.7 fusion.45
  9.6 0.7 fusion.46
  10.3 0.7 copy.9
  11.2 0.1 reduce
  11.3 0.7 sub.6
  11.9 0.7 fusion.51
  12.6 0.7 fusion.48
  13.3 0.7 fusion.49
  14.1 0.7 fusion.50
  14.8 0.8 convert_reduce_fusion
  15.6 4.3 %compare_select_fusion.2 = (s32[512,1]{0,1:T(1,128)S(1)}, s32[512,1]{0,1:T(1,128)S(1)}) fusion(s32[]{:T(128)} %bitcast.59, s32[]{:T(128)} %bitcast.60, s32[]{:T(128)} %bitcast.61, s32[]{:T(128)} %bitcast.62, s32[]{:T(128)} %bitcast.63, s32[]{:T(128)} %bitcast.65, s32[]{:T(128)} %bitcast.64, s32[512,1]{0,1:T(1,128)S(1)} %bitcast.136), kind=kLoop, calls=%fused_computation.85 | loop fusion | flops 7680 | bytes 6172 | tf_op jit(solution)/shard_map/gather | solution.py:16
  19.9 0.4 compare_reduce_fusion.56
  20.3 4.4 %compare_select_fusion.3 = s32[512,1]{0,1:T(1,128)S(1)} fusion(s32[512,1]{0,1:T(1,128)S(1)} %get-tuple-element.63, s32[]{:T(128)} %bitcast.124, s32[]{:T(128)} %bitcast.125, s32[]{:T(128)} %bitcast.126, s32[]{:T(128)} %bitcast.127, s32[]{:T(128)} %bitcast.128, s32[]{:T(128)} %bitcast.130, s32[]{:T(128)} %bitcast.129), kind=kLoop, calls=%fused_computation.86 | loop fusion | flops 6144 | bytes 4124 | tf_op jit(solution)/shard_map/gather | solution.py:16
  24.7 72.0 %compare_select_fusion.1 = s32[512]{0:T(512)S(1)} fusion(pred[512]{0:T(512)(128)(4,1)S(1)} %get-tuple-element.61, pred[512]{0:T(512)(128)(4,1)S(1)} %get-tuple-element.60, pred[512]{0:T(512)(128)(4,1)S(1)} %get-tuple-element.59, pred[512]{0:T(512)(128)(4,1)S(1)} %get-tuple-element.58, pred[512]{0:T(512)(128)(4,1)S(1)} %get-tuple-element.57, ...), kind=kLoop, calls=%fused_computation.84 | loop fusion | flops 60928 | bytes 37832 | tf_op jit(solution)/shard_map/select_n | solution.py:22
  96.7 15.6 %all_gather.3 = bf16[512,928]{1,0:T(8,128)(2,1)S(1)} all-gather(bf16[64,928]{1,0:T(8,128)(2,1)} %param.6), channel_id=1, replica_groups=mesh['gr'=8,'gc'=8,'dr'=2] {'gr'}, dimensions={0}, use_global_device_ids=true | all-gather | bytes 1069056 | tf_op jit(solution)/shard_map/all_gather | solution.py:20
  112.3 2.1 gather_fusion
  114.3 14.8 %fusion.52 = f32[512,6656]{1,0:T(8,128)} fusion(bf16[512,928]{1,0:T(8,128)(2,1)S(1)} %gather_fusion, bf16[928,6656]{1,0:T(8,128)(2,1)} %param.10), kind=kOutput, calls=%fused_computation.138 | convolution fusion | flops 6325010432 | bytes 26935296 | tf_op jit(solution)/shard_map/dot_general | solution.py:23
  129.2 190.2 %all-reduce.2.cloned.1.call-done = f32[512,6656]{1,0:T(8,128)} async-done(((f32[512,6656]{1,0:T(8,128)}), f32[512,6656]{1,0:T(8,128)}) %all-reduce.2.cloned.1.call-update) | async-done | bytes 13631504 | tf_op jit(solution)/shard_map/psum | solution.py:24
  319.4 41.1 %fusion.10 = f32[512,928]{1,0:T(8,128)} fusion(bf16[6656,928]{0,1:T(8,128)(2,1)} %param.11, f32[512,6656]{1,0:T(8,128)} %all-reduce.2.cloned.1.call-done), kind=kOutput, calls=%fused_computation.20 | convolution fusion | flops 6546522112 | bytes 27885568 | tf_op jit(solution)/shard_map/dot_general | solution.py:27
  360.6 30.5 %reduce-scatter.2.cloned.1.call-done = f32[64,928]{1,0:T(8,128)} async-done(((f32[512,928]{1,0:T(8,128)}), f32[64,928]{1,0:T(8,128)}) %reduce-scatter.2.cloned.1.call-update) | async-done | bytes 237584 | tf_op jit(solution)/shard_map/reduce_scatter | solution.py:26
  391.1 1.6 convert_element_type.11
  (6 shorter events, 0.2 us)
Async XLA Ops:
  6.5 312.9 %all-reduce.2.cloned.1.call-start = ((), (), s32[]{:S(2)}) async-start(), calls=%async_computation.1 | async-start | bytes 27262976 | tf_op jit(solution)/shard_map/psum | solution.py:24
  129.2 261.9 %reduce-scatter.2.cloned.1.call-start = ((), (), s32[]{:S(2)}) async-start(), calls=%async_computation.2 | async-start | bytes 2359296 | tf_op jit(solution)/shard_map/reduce_scatter | solution.py:26
Sparse Core Ops, SparseCore 0:
  129.3 190.1 all-reduce.1
  360.7 30.3 reduce-scatter.1
where the time goes:
time: 403 us; the launch traced here: 400 us
  waiting for transfers between devices  221 us (55%)
  other arithmetic  85.3 us (21%)
  matrix products  55.9 us (14%)
  blocking collectives  15.6 us (4%)
  between operations  13.5 us (3%)
  local copies, waits for them, and re-layouts  8.51 us (2%)
    psum x1, waiting for transfers between devices, on_device(): pre = lax.psum(partial_value, ('gc', 'dr'))  190 us
    select_n x1, other arithmetic, on_device(): candidates = gathered[source]  72 us
    dot_general x1, matrix products, on_device(): jnp.dot(hidden, down_weight, preferred_element_type=jnp.float32)  41.1 us
    reduce_scatter x1, waiting for transfers between devices, on_device(): lax.psum_scatter(jnp.dot(hidden, down_weight, preferred_element_type=jnp....  30.5 us
    all_gather x1, blocking collectives, on_device(): gathered = lax.all_gather(draft_rows, 'gr', axis=0, tiled=True)  15.6 us
    dot_general x1, matrix products, on_device(): jnp.dot(candidates, up_weight, preferred_element_type=jnp.float32)  14.8 us
    gather x3, other arithmetic, source_rows(): return draft_start[owner] + row_order - req_start[owner]  9.09 us
  transfers between devices with their start and end apart: 2, of which 2 were waited for; matrix products, arithmetic and copies ran while one was open for 0% of the time, Pallas kernels for 0%

commit v1 on v0

v1 whole, which is shorter than its diff:
```python
import functools

import jax
import jax.numpy as jnp
from jax import lax
from jax.experimental import pallas as pl
from jax.experimental.pallas import tpu as pltpu
from jax.sharding import PartitionSpec as P

BF, F32 = jnp.bfloat16, jnp.float32
YZ = ("gc", "dr")
LIMIT = 8 << 20


def place(y, z):
    return (y * 2 + z % 2) * 2 + z // 2


SIDES = ((1, 0, 3, 2), (3, 2, 1, 0))
SWAPS = tuple(
    [(place(y, z), place(side[y], z)) for y in range(4) for z in range(4)] for side in SIDES
) + tuple(
    [(place(y, z), place(y, side[z])) for y in range(4) for z in range(4)] for side in SIDES
)


def swap(value, side):
    return lax.ppermute(value, YZ, SWAPS[side])


def from_chip(value, ahead):
    pairs = [(((x + ahead) % 4) * 2 + c, x * 2 + c) for x in range(4) for c in range(2)]
    return lax.ppermute(value, "gr", pairs)


def other_core(value):
    return lax.ppermute(value, "gr", [(i, i ^ 1) for i in range(8)])


def square_bits(p):
    return (p & 1) ^ (p >> 1), p >> 1


def run(kernel, outs, *args, spaces=None, flops=0, moved=0, erfs=0, aliases=None, scratch=()):
    vmem = pl.BlockSpec(memory_space=pltpu.VMEM)
    specs = [vmem] * len(args)
    for i, space in (spaces or {}).items():
        specs[i] = pl.BlockSpec(memory_space=space)
    single = not isinstance(outs, list)
    shapes = [outs] if single else outs
    moved = moved or sum(a.size * a.dtype.itemsize for a in args)
    out = pl.pallas_call(
        kernel,
        out_shape=shapes,
        in_specs=specs,
        out_specs=[vmem] * len(shapes),
        scratch_shapes=list(scratch),
        input_output_aliases=aliases or {},
        compiler_params=pltpu.CompilerParams(vmem_limit_bytes=LIMIT),
        cost_estimate=pl.CostEstimate(flops=flops, bytes_accessed=moved, transcendentals=erfs),
    )(*args)
    return out[0] if single else out


def load_kernel(count, *refs):
    src, extras = refs[0], refs[1 : 1 + count]
    out, extra_outs, sems = refs[-2 - count], refs[-1 - count : -1], refs[-1]
    width = out.shape[2]
    copies = [
        pltpu.make_async_copy(src.at[:, pl.ds(i * width, width)], out.at[i], sems.at[i])
        for i in range(4)
    ]
    for i in range(count):
        copies.append(pltpu.make_async_copy(extras[i], extra_outs[i], sems.at[4 + i]))
    for copy in copies:
        copy.start()
    for copy in copies:
        copy.wait()


def load(weight, *extras, after=None):
    rows, columns = weight.shape
    count = len(extras)
    values = [pltpu.with_memory_space_constraint(v, pltpu.HBM) for v in (weight, *extras)]
    spaces = {i: pltpu.HBM for i in range(1 + count)}
    if after is not None:
        values.append(after)
        spaces[1 + count] = pl.ANY
    out = run(
        functools.partial(load_kernel, count),
        [pltpu.VMEM((4, rows, columns // 4), BF)] + [pltpu.VMEM(v.shape, v.dtype) for v in extras],
        *values,
        spaces=spaces,
        moved=weight.size * 4,
        scratch=[pltpu.SemaphoreType.DMA((4 + count,))],
    )
    return out if extras else out[0]


def pack_kernel(*refs):
    out, at = refs[-1], 0
    for ref in refs[:-1]:
        out[at : at + ref.shape[0]] = ref[...]
        at += ref.shape[0]


def pack(*values):
    rows = sum(v.shape[0] for v in values)
    return run(pack_kernel, pltpu.VMEM((rows, values[0].shape[1]), BF), *values)


def side_bit(ids, side):
    return (square_bits(ids[1] >> 1) + square_bits(ids[2] * 2 + (ids[1] & 1)))[side % 4]


def quarter_of(ids, q, far):
    return (q % 2) * 2 + (side_bit(ids, q) ^ far)


def half_of(ids, q, near, rows):
    return pl.ds(pl.multiple_of((side_bit(ids, q + 1) ^ near) * rows, rows), rows)


def up_kernel(q, far, ids, rows_ref, weight_ref, after, out_ref):
    half = out_ref.shape[0] // 2
    rows = jnp.concatenate([rows_ref[half_of(ids, q, near, half)] for near in range(2)])
    quarter = quarter_of(ids, q, far)
    width = weight_ref.shape[2]
    for start in range(0, width, 256):
        stop = min(start + 256, width)
        value = jnp.dot(rows, weight_ref[quarter, :, start:stop], preferred_element_type=F32)
        out_ref[:, start:stop] = value.astype(out_ref.dtype)


def second_kernel(kept_ref, got_ref, after, out_ref):
    n = out_ref.shape[0]
    out_ref[...] = (kept_ref[n:] + got_ref[n:].astype(F32)).astype(BF)


def third_kernel(kept_ref, got_ref, new_ref, sum_ref, out_ref):
    n = out_ref.shape[0]
    value = kept_ref[:n] + got_ref[:n].astype(F32) + new_ref[...].astype(F32)
    sum_ref[...] = value
    out_ref[...] = value.astype(BF)


def fourth_kernel(kept_ref, got_ref, sum_ref, out_ref):
    value = kept_ref[...] + got_ref[...].astype(F32)
    sum_ref[...] = value
    out_ref[...] = value.astype(BF)


def gelu_kernel(kept_ref, got_ref, out_ref):
    value = kept_ref[...] + got_ref[...].astype(F32)
    value = value * (1.0 + lax.erf(value * (2.0**-0.5))) * 0.5
    out_ref[...] = value.astype(BF)


def add_down(ids, q, far, rows_ref, weight_ref, from_ref, out_ref):
    half = out_ref.shape[0] // 2
    value = lax.dot_general(
        rows_ref[...],
        weight_ref[quarter_of(ids, q, far)],
        (((1,), (1,)), ((), ())),
        preferred_element_type=F32,
    )
    for near in range(2):
        at = half_of(ids, q, near, half)
        rows = value[near * half : (near + 1) * half]
        out_ref[at] = rows if from_ref is None else from_ref[at] + rows


def down_own_kernel(q, ids, one_ref, two_ref, weight_ref, out_ref):
    add_down(ids, q, 0, one_ref, weight_ref, None, out_ref)
    add_down(ids, q + 1, 0, two_ref, weight_ref, out_ref, out_ref)


def down_kernel(q, ids, total_ref, rows_ref, weight_ref, out_ref):
    add_down(ids, q, 1, rows_ref, weight_ref, total_ref, out_ref)


def index_kernel(ids, sizes_ref, map_ref, order_ref, after, out_ref, mid_ref):
    rows = order_ref.shape[1]
    reqs = sizes_ref.shape[1]
    own = rows // 8
    down_at = lax.broadcasted_iota(jnp.int32, (reqs, reqs), 0)
    along = lax.broadcasted_iota(jnp.int32, (reqs, reqs), 1)
    sizes, owner = sizes_ref[...], map_ref[...]

    def upright(row):
        return jnp.sum(jnp.where(down_at == along, row, 0), axis=1, keepdims=True)

    earlier = along < down_at
    owners = upright(owner)
    before = (owner < owners) | ((owner == owners) & earlier)
    start = jnp.sum(jnp.where(earlier, sizes, 0), axis=1, keepdims=True)
    shift = jnp.sum(jnp.where(before, sizes, 0), axis=1, keepdims=True) - start
    order = order_ref[...]
    inside = (order >= start) & (order < start + upright(sizes))
    source = order + jnp.sum(jnp.where(inside, shift, 0), axis=0, keepdims=True)
    chip, core = ids[0] >> 1, ids[0] & 1
    ahead = (source // (2 * own) - chip) & 3
    slot = jnp.where(ahead == 2, 1, jnp.where(ahead == 1, 2, ahead))
    at = (((source // own) & 1) ^ core) * (4 * own) + slot * own + source % own
    spots = lax.broadcasted_iota(jnp.int32, (rows, rows), 0)
    mid_ref[...] = jnp.where(spots == at, 1.0, 0.0).T.astype(BF)
    for t in range(8):
        block = ((t + chip) & 3) * 2 + ((t // 4) ^ core)
        out_ref[t * own : (t + 1) * own] = mid_ref[pl.ds(pl.multiple_of(block * own, own), own)]


def sort_kernel(at, pick_ref, value_ref, *refs):
    kept_ref, out_ref = refs[-2:]
    half = kept_ref.shape[0]
    value = value_ref[...]
    high = value.astype(BF)
    low = (value - high.astype(F32)).astype(BF)
    pick = pick_ref[:, at : at + value.shape[0]]
    kept = jnp.dot(pick[:half], high, preferred_element_type=F32)
    kept += jnp.dot(pick[:half], low, preferred_element_type=F32)
    out = jnp.dot(pick[half:], high, preferred_element_type=F32)
    if len(refs) == 4:
        kept += refs[0][...]
        out += refs[1][...]
    kept_ref[...] = kept
    out_ref[...] = out.astype(out_ref.dtype)


def deal_kernel(kept_ref, got_ref, mine_ref, *out_refs):
    n = mine_ref.shape[0]
    mine_ref[...] = kept_ref[:n] + got_ref[:n].astype(F32)
    for i, out_ref in enumerate(out_refs):
        at = slice((i + 1) * n, (i + 2) * n)
        out_ref[...] = (kept_ref[at] + got_ref[at].astype(F32)).astype(BF)


def last_kernel(mine_ref, *refs):
    value = mine_ref[...]
    for ref in refs[:-1]:
        value += ref[...].astype(F32)
    refs[-1][...] = value.astype(BF)


def on_device(draft_rows, tree_sizes, draft_map, row_order, up_weight, down_weight):
    own, width = draft_rows.shape
    rows, hidden_units = row_order.shape[0], up_weight.shape[1]
    part = hidden_units // 4
    group = rows // 2
    chains = range(4)
    ids = jnp.stack([lax.axis_index("gr"), lax.axis_index("gc"), lax.axis_index("dr")])
    ids = ids.astype(jnp.int32)
    smem = pltpu.SMEM

    fetched = [from_chip(draft_rows, ahead) for ahead in (2, 1, 3)]
    ups, draft = load(up_weight, draft_rows)
    column = pack(draft, *fetched)
    beside = other_core(column)

    project_flops = 2 * group * width * part

    def project(q, far, dtype, after):
        return run(
            functools.partial(up_kernel, q, far),
            pltpu.VMEM((group, part), dtype),
            ids,
            column if q < 2 else beside,
            ups,
            after,
            spaces={0: smem, 3: pl.ANY},
            flops=project_flops,
        )

    sent, after = [], column
    for q in chains:
        after = project(q, 1, BF, after)
        sent.append(after)
    got = [swap(sent[q], q) for q in chains]
    kept = []
    for q in chains:
        after = project(q, 0, F32, after)
        kept.append(after)
    pick = run(
        index_kernel,
        pltpu.VMEM((rows, rows), BF),
        ids,
        tree_sizes[None, :],
        draft_map[None, :],
        row_order[None, :],
        after,
        spaces={0: smem, 4: pl.ANY},
        flops=rows * rows * 64,
        scratch=[pltpu.VMEM((rows, rows), BF)],
    )
    downs = load(down_weight.T, after=after)

    block = pltpu.VMEM((group // 2, part), BF)
    block32 = pltpu.VMEM((group // 2, part), F32)
    came = [
        swap(run(second_kernel, block, kept[q], got[q], after, spaces={2: pl.ANY}), (q + 1) % 4)
        for q in chains
    ]
    third = [run(third_kernel, [block32, block], kept[q], got[q], came[q]) for q in chains]
    came = [swap(third[q][1], (q + 2) % 4) for q in chains]
    fourth = [run(fourth_kernel, [block32, block], third[q][0], came[q]) for q in chains]
    came = [swap(fourth[q][1], (q + 3) % 4) for q in chains]
    erfs = group // 2 * part
    hidden = [run(gelu_kernel, block, fourth[q][0], came[q], erfs=erfs) for q in chains]
    came = [swap(hidden[q], (q + 1) % 4) for q in chains]
    mine = [pack(hidden[q], came[q]) for q in chains]
    came = [swap(mine[q], q) for q in chains]
    whole = pltpu.VMEM((group, width), F32)
    sorted_rows = []
    for i in range(2):
        total = run(
            functools.partial(down_own_kernel, 2 * i),
            whole,
            ids,
            mine[2 * i],
            mine[2 * i + 1],
            downs,
            spaces={0: smem},
            flops=2 * project_flops,
        )
        for q in (2 * i, 2 * i + 1):
            total = run(
                functools.partial(down_kernel, q),
                whole,
                ids,
                total,
                came[q],
                downs,
                spaces={0: smem},
                flops=project_flops,
            )
        sorted_rows = run(
            functools.partial(sort_kernel, i * group),
            [whole, pltpu.VMEM((group, width), BF if i else F32)],
            pick,
            total,
            *sorted_rows,
            flops=3 * group * group * width,
        )
    kept, out = sorted_rows
    row_block = pltpu.VMEM((own, width), BF)
    mine, one, two, three = run(
        deal_kernel,
        [pltpu.VMEM((own, width), F32), row_block, row_block, row_block],
        kept,
        other_core(out),
    )
    arrived = [from_chip(value, ahead) for ahead, value in ((2, two), (1, three), (3, one))]
    return run(last_kernel, jax.ShapeDtypeStruct((own, width), BF), mine, *arrived)


def solution(mesh):
    return jax.shard_map(
        on_device,
        mesh=mesh,
        in_specs=(
            P("gr", ("gc", "dr")),
            P(),
            P(),
            P(),
            P(("gc", "dr"), "gr"),
            P("gr", ("gc", "dr")),
        ),
        out_specs=P("gr", ("gc", "dr")),
        check_vma=False,
    )
```

time: 403 us -> 138 us (0.34)
  waiting for transfers between devices: 221 us -> 41.9 us
  other arithmetic: 85.3 us -> 0.08 us
  matrix products: 55.9 us -> 0 us
  starting transfers between devices: 0.04 us -> 46.2 us
  Pallas kernels: 0 us -> 40.5 us
  blocking collectives: 15.6 us -> 0 us
  between operations: 13.5 us -> 0.35 us
    psum x1 -> x0, waiting for transfers between devices: 190 us -> none  [on_device(): pre = lax.psum(partial_value, ('gc', 'dr'))]
    select_n x1 -> x0, other arithmetic: 72 us -> none  [on_device(): candidates = gathered[source]]
    dot_general x2 -> x0, matrix products: 55.9 us -> none  [the longest x1 41.1 us: on_device(): jnp.dot(hidden, down_weight, preferred_element_type=jnp.float32)]
    ppermute x0 -> x32, starting transfers between devices: none -> 46.2 us  [the longest x24 34.5 us: swap(): return lax.ppermute(value, YZ, SWAPS[side])]
    ppermute x0 -> x32, waiting for transfers between devices: none -> 41.9 us  [the longest x24 32.4 us: swap(): return lax.ppermute(value, YZ, SWAPS[side])]
    pallas_call x0 -> x42, Pallas kernels: none -> 40.5 us  [run(): pl.pallas_call(kernel, out_shape=shapes, in_specs=specs, out_specs=[vmem]...]
    reduce_scatter x1 -> x0, waiting for transfers between devices: 30.5 us -> none  [on_device(): lax.psum_scatter(jnp.dot(hidden, down_weight, preferred_element_type=jnp....]
    all_gather x1 -> x0, blocking collectives: 15.6 us -> none  [on_device(): gathered = lax.all_gather(draft_rows, 'gr', axis=0, tiled=True)]
  transfers between devices with their start and end apart: 2 -> 32, of which waited for: 2 -> 17; matrix products, arithmetic and copies ran while one was open for 0% -> 0% of each run, Pallas kernels for 0% -> 27%
where the time goes in v1:
time: 138 us
  starting transfers between devices  46.2 us (33%)
  waiting for transfers between devices  41.9 us (30%)
  Pallas kernels  40.5 us (29%)
  local copies, waits for them, and re-layouts  8.95 us (6%)
    pallas_call x42, Pallas kernels, run(): pl.pallas_call(kernel, out_shape=shapes, in_specs=specs, out_specs=[vmem]...  40.5 us
    ppermute x24, starting transfers between devices, swap(): return lax.ppermute(value, YZ, SWAPS[side])  34.5 us
    ppermute x24, waiting for transfers between devices, swap(): return lax.ppermute(value, YZ, SWAPS[side])  32.4 us
    unnamed x10, local copies, waits for them, and re-layouts  8.95 us
    ppermute x6, waiting for transfers between devices, from_chip(): return lax.ppermute(value, 'gr', pairs)  7.99 us
    ppermute x6, starting transfers between devices, from_chip(): return lax.ppermute(value, 'gr', pairs)  7.87 us
    ppermute x2, starting transfers between devices, other_core(): return lax.ppermute(value, 'gr', [(i, i ^ 1) for i in range(8)])  3.78 us
  transfers between devices with their start and end apart: 32, of which 17 were waited for; matrix products, arithmetic and copies ran while one was open for 0% of the time, Pallas kernels for 27%

profile of v1, /device:TPU:1, one launch (start us, length us, event | category | flops | bytes accessed | tf_op | source)
XLA Modules:
  0.0 137.9 jit_solution(6805305280795915882)
XLA Ops:
  0.0 3.6 %collective-permute-start = (bf16[64,928]{1,0:T(8,128)(2,1)}, bf16[64,928]{1,0:T(8,128)(2,1)S(1)}, u32[]{:S(2)}, u32[]{:S(2)}) collective-permute-start(bf16[64,928]{1,0:T(8,128)(2,1)} %refs_1_.1), channel_id=1, source_target_pairs={{64,0},{80,16},{96,32},{112,48},{0,64},{16,80},{32,96},{48,112},{6... | collective-permute-start | bytes 356360 | tf_op jit(solution)/shard_map/ppermute | solution.py:33
  3.9 2.4 %collective-permute-start.1 = (bf16[64,928]{1,0:T(8,128)(2,1)}, bf16[64,928]{1,0:T(8,128)(2,1)S(1)}, u32[]{:S(2)}, u32[]{:S(2)}) collective-permute-start(bf16[64,928]{1,0:T(8,128)(2,1)} %refs_1_.1), channel_id=1, source_target_pairs={{32,0},{48,16},{64,32},{80,48},{96,64},{112,80},{0,96},{16,112},{3... | collective-permute-start | bytes 356360 | tf_op jit(solution)/shard_map/ppermute | solution.py:33
  6.3 4.7 %shard_map.64 = (bf16[4,928,1664]{2,1,0:T(8,128)(2,1)S(1)}, bf16[64,928]{1,0:T(8,128)(2,1)S(1)}) custom-call(bf16[928,6656]{1,0:T(8,128)(2,1)} %refs_0_.1, bf16[64,928]{1,0:T(8,128)(2,1)} %refs_1_.1), custom_call_target="tpu_custom_call" | custom-call | bytes 24707072 | tf_op jit(solution)/shard_map/pallas_call | solution.py:52
  10.9 4.4 %copy-done = bf16[4,928,1664]{2,1,0:T(8,128)(2,1)} copy-done((bf16[4,928,1664]{2,1,0:T(8,128)(2,1)}, bf16[4,928,1664]{2,1,0:T(8,128)(2,1)S(1)}, u32[]{:S(2)}) %copy-start) | copy-done | bytes 12353560
  17.1 4.5 %copy-done.1 = bf16[4,928,1664]{2,1,0:T(8,128)(2,1)S(1)} copy-done((bf16[4,928,1664]{2,1,0:T(8,128)(2,1)S(1)}, bf16[4,928,1664]{2,1,0:T(8,128)(2,1)}, u32[]{:S(2)}) %copy-start.1) | copy-done | bytes 12353560
  26.3 2.0 %collective-permute-start.21 = (bf16[256,1664]{1,0:T(8,128)(2,1)S(1)}, bf16[256,1664]{1,0:T(8,128)(2,1)S(1)}, u32[]{:S(2)}, u32[]{:S(2)}) collective-permute-start(bf16[256,1664]{1,0:T(8,128)(2,1)S(1)} %shard_map.67.after), channel_id=1, source_target_pairs={{0,12},{2,14},{1,13},{3,15},{4,8},{6,10},{5,9},{7,11},{8,4},{10,6}... | collective-permute-start | bytes 2555912 | tf_op jit(solution)/shard_map/ppermute | solution.py:28
  33.3 2.3 %collective-permute-start.9 = (bf16[256,1664]{1,0:T(8,128)(2,1)S(1)}, bf16[256,1664]{1,0:T(8,128)(2,1)S(1)}, u32[]{:S(2)}, u32[]{:S(2)}) collective-permute-start(bf16[256,1664]{1,0:T(8,128)(2,1)S(1)} %shard_map.69.after), channel_id=1, source_target_pairs={{0,3},{2,1},{1,2},{3,0},{4,7},{6,5},{5,6},{7,4},{8,11},{10,9},{9,1... | collective-permute-start | bytes 2555912 | tf_op jit(solution)/shard_map/ppermute | solution.py:28
  44.0 2.8 %collective-permute-start.17 = (bf16[128,1664]{1,0:T(8,128)(2,1)S(1)}, bf16[128,1664]{1,0:T(8,128)(2,1)S(1)}, u32[]{:S(2)}, u32[]{:S(2)}) collective-permute-start(bf16[128,1664]{1,0:T(8,128)(2,1)S(1)} %shard_map.89), channel_id=1, source_target_pairs={{0,12},{2,14},{1,13},{3,15},{4,8},{6,10},{5,9},{7,11},{8,4},{10,6}... | collective-permute-start | bytes 1277960 | tf_op jit(solution)/shard_map/ppermute | solution.py:28
  47.9 1.7 %collective-permute-start.22 = (bf16[128,1664]{1,0:T(8,128)(2,1)S(1)}, bf16[128,1664]{1,0:T(8,128)(2,1)S(1)}, u32[]{:S(2)}, u32[]{:S(2)}) collective-permute-start(bf16[128,1664]{1,0:T(8,128)(2,1)S(1)} %shard_map.94), channel_id=1, source_target_pairs={{0,2},{2,0},{1,3},{3,1},{4,6},{6,4},{5,7},{7,5},{8,10},{10,8},{9,1... | collective-permute-start | bytes 1277960 | tf_op jit(solution)/shard_map/ppermute | solution.py:28
  50.4 3.5 %collective-permute-start.5 = (bf16[128,1664]{1,0:T(8,128)(2,1)S(1)}, bf16[128,1664]{1,0:T(8,128)(2,1)S(1)}, u32[]{:S(2)}, u32[]{:S(2)}) collective-permute-start(bf16[128,1664]{1,0:T(8,128)(2,1)S(1)} %shard_map.75), channel_id=1, source_target_pairs={{0,3},{2,1},{1,2},{3,0},{4,7},{6,5},{5,6},{7,4},{8,11},{10,9},{9,1... | collective-permute-start | bytes 1277960 | tf_op jit(solution)/shard_map/ppermute | solution.py:28
  54.8 2.2 %collective-permute-done.17.new_ref = bf16[128,1664]{1,0:T(8,128)(2,1)S(1)} collective-permute-done((bf16[128,1664]{1,0:T(8,128)(2,1)S(1)}, bf16[128,1664]{1,0:T(8,128)(2,1)S(1)}, u32[]{:S(2)}, u32[]{:S(2)}) %collective-permute-start.17) | collective-permute-done | bytes 426016 | tf_op jit(solution)/shard_map/ppermute | solution.py:28
  59.0 3.3 %collective-permute-start.23 = (bf16[128,1664]{1,0:T(8,128)(2,1)S(1)}, bf16[128,1664]{1,0:T(8,128)(2,1)S(1)}, u32[]{:S(2)}, u32[]{:S(2)}) collective-permute-start(bf16[128,1664]{1,0:T(8,128)(2,1)S(1)} %get-tuple-element.46), channel_id=1, source_target_pairs={{0,3},{2,1},{1,2},{3,0},{4,7},{6,5},{5,6},{7,4},{8,11},{10,9},{9,1... | collective-permute-start | bytes 1277960 | tf_op jit(solution)/shard_map/ppermute | solution.py:28
  65.3 2.9 %collective-permute-done.18.got_ref = bf16[128,1664]{1,0:T(8,128)(2,1)S(1)} collective-permute-done((bf16[128,1664]{1,0:T(8,128)(2,1)S(1)}, bf16[128,1664]{1,0:T(8,128)(2,1)S(1)}, u32[]{:S(2)}, u32[]{:S(2)}) %collective-permute-start.18) | collective-permute-done | bytes 426016 | tf_op jit(solution)/shard_map/ppermute | solution.py:28
  68.3 3.5 %collective-permute-start.19 = (bf16[128,1664]{1,0:T(8,128)(2,1)S(1)}, bf16[128,1664]{1,0:T(8,128)(2,1)S(1)}, u32[]{:S(2)}, u32[]{:S(2)}) collective-permute-start(bf16[128,1664]{1,0:T(8,128)(2,1)S(1)} %get-tuple-element.44), channel_id=1, source_target_pairs={{0,3},{2,1},{1,2},{3,0},{4,7},{6,5},{5,6},{7,4},{8,11},{10,9},{9,1... | collective-permute-start | bytes 1277960 | tf_op jit(solution)/shard_map/ppermute | solution.py:28
  74.9 6.8 %collective-permute-done.19.got_ref = bf16[128,1664]{1,0:T(8,128)(2,1)S(1)} collective-permute-done((bf16[128,1664]{1,0:T(8,128)(2,1)S(1)}, bf16[128,1664]{1,0:T(8,128)(2,1)S(1)}, u32[]{:S(2)}, u32[]{:S(2)}) %collective-permute-start.19) | collective-permute-done | bytes 426016 | tf_op jit(solution)/shard_map/ppermute | solution.py:28
  86.2 8.2 %collective-permute-done.20.refs_1_ = bf16[128,1664]{1,0:T(8,128)(2,1)S(1)} collective-permute-done((bf16[128,1664]{1,0:T(8,128)(2,1)S(1)}, bf16[128,1664]{1,0:T(8,128)(2,1)S(1)}, u32[]{:S(2)}, u32[]{:S(2)}) %collective-permute-start.20) | collective-permute-done | bytes 426016 | tf_op jit(solution)/shard_map/ppermute | solution.py:28
  96.7 2.1 %collective-permute-start.15 = (bf16[256,1664]{1,0:T(8,128)(2,1)S(1)}, bf16[256,1664]{1,0:T(8,128)(2,1)S(1)}, u32[]{:S(2)}, u32[]{:S(2)}) collective-permute-start(bf16[256,1664]{1,0:T(8,128)(2,1)S(1)} %shard_map.84.two_ref), channel_id=1, source_target_pairs={{0,3},{2,1},{1,2},{3,0},{4,7},{6,5},{5,6},{7,4},{8,11},{10,9},{9,1... | collective-permute-start | bytes 2555912 | tf_op jit(solution)/shard_map/ppermute | solution.py:28
  98.9 4.7 %shard_map.85.weight_ref = bf16[4,928,1664]{2,1,0:T(8,128)(2,1)S(1)} custom-call(bf16[928,6656]{1,0:T(8,128)(2,1)} %bitcast.10, f32[256,1664]{1,0:T(8,128)S(1)} %shard_map.73.after.kept_ref.refs_1_), custom_call_target="tpu_custom_call" | custom-call | bytes 24707072 | tf_op jit(solution)/shard_map/pallas_call | solution.py:52
  104.6 2.6 %shard_map.99.total_ref = f32[256,928]{1,0:T(8,128)S(1)} custom-call(s32[3]{0:T(128)S(1)} %pad_add_fusion.ids, bf16[256,1664]{1,0:T(8,128)(2,1)S(1)} %shard_map.93.one_ref, bf16[256,1664]{1,0:T(8,128)(2,1)S(1)} %shard_map.98.two_ref, bf16[4,928,1664]{2,1,0:T(8,128)(2,1)S(1)} %shard_map.85.weight_ref), custom_call_target="tpu_custom_call" | custom-call | flops 1581252608 | bytes 14057484 | tf_op jit(solution)/shard_map/pallas_call | solution.py:52
  107.3 2.7 %shard_map.86.total_ref = f32[256,928]{1,0:T(8,128)S(1)} custom-call(s32[3]{0:T(128)S(1)} %pad_add_fusion.ids, bf16[256,1664]{1,0:T(8,128)(2,1)S(1)} %shard_map.79.one_ref, bf16[256,1664]{1,0:T(8,128)(2,1)S(1)} %shard_map.84.two_ref, bf16[4,928,1664]{2,1,0:T(8,128)(2,1)S(1)} %shard_map.85.weight_ref), custom_call_target="tpu_custom_call" | custom-call | flops 1581252608 | bytes 14057484 | tf_op jit(solution)/shard_map/pallas_call | solution.py:52
  109.9 5.7 %collective-permute-done.26.rows_ref = bf16[256,1664]{1,0:T(8,128)(2,1)S(1)} collective-permute-done((bf16[256,1664]{1,0:T(8,128)(2,1)S(1)}, bf16[256,1664]{1,0:T(8,128)(2,1)S(1)}, u32[]{:S(2)}, u32[]{:S(2)}) %collective-permute-start.26) | collective-permute-done | bytes 852000 | tf_op jit(solution)/shard_map/ppermute | solution.py:28
  123.7 2.2 %collective-permute-start.28 = (bf16[256,928]{1,0:T(8,128)(2,1)S(1)}, bf16[256,928]{1,0:T(8,128)(2,1)S(1)}, u32[]{:S(2)}, u32[]{:S(2)}) collective-permute-start(bf16[256,928]{1,0:T(8,128)(2,1)S(1)} %get-tuple-element.52), channel_id=1, source_target_pairs={{0,16},{16,0},{32,48},{48,32},{64,80},{80,64},{96,112},{112,96},{1... | collective-permute-start | bytes 1425416 | tf_op jit(solution)/shard_map/ppermute | solution.py:37
  129.2 4.7 %collective-permute-done.29.refs_0_ = bf16[64,928]{1,0:T(8,128)(2,1)S(1)} collective-permute-done((bf16[64,928]{1,0:T(8,128)(2,1)S(1)}, bf16[64,928]{1,0:T(8,128)(2,1)S(1)}, u32[]{:S(2)}, u32[]{:S(2)}) %collective-permute-start.29) | collective-permute-done | bytes 118816 | tf_op jit(solution)/shard_map/ppermute | solution.py:33
  134.0 3.2 %collective-permute-done.31.refs_2_ = bf16[64,928]{1,0:T(8,128)(2,1)S(1)} collective-permute-done((bf16[64,928]{1,0:T(8,128)(2,1)S(1)}, bf16[64,928]{1,0:T(8,128)(2,1)S(1)}, u32[]{:S(2)}, u32[]{:S(2)}) %collective-permute-start.31) | collective-permute-done | bytes 118816 | tf_op jit(solution)/shard_map/ppermute | solution.py:33
  (93 shorter events, 51.0 us)
Async XLA Ops:
  0.0 15.4 %collective-permute-start = (bf16[64,928]{1,0:T(8,128)(2,1)}, bf16[64,928]{1,0:T(8,128)(2,1)S(1)}, u32[]{:S(2)}, u32[]{:S(2)}) collective-permute-start(bf16[64,928]{1,0:T(8,128)(2,1)} %refs_1_.1), channel_id=1, source_target_pairs={{64,0},{80,16},{96,32},{112,48},{0,64},{16,80},{32,96},{48,112},{6... | collective-permute-start | bytes 356360 | tf_op jit(solution)/shard_map/ppermute | solution.py:33
  3.6 11.8 %collective-permute-start.2 = (bf16[64,928]{1,0:T(8,128)(2,1)}, bf16[64,928]{1,0:T(8,128)(2,1)S(1)}, u32[]{:S(2)}, u32[]{:S(2)}) collective-permute-start(bf16[64,928]{1,0:T(8,128)(2,1)} %refs_1_.1), channel_id=1, source_target_pairs={{96,0},{112,16},{0,32},{16,48},{32,64},{48,80},{64,96},{80,112},{9... | collective-permute-start | bytes 356360 | tf_op jit(solution)/shard_map/ppermute | solution.py:33
  3.9 11.5 %collective-permute-start.1 = (bf16[64,928]{1,0:T(8,128)(2,1)}, bf16[64,928]{1,0:T(8,128)(2,1)S(1)}, u32[]{:S(2)}, u32[]{:S(2)}) collective-permute-start(bf16[64,928]{1,0:T(8,128)(2,1)} %refs_1_.1), channel_id=1, source_target_pairs={{32,0},{48,16},{64,32},{80,48},{96,64},{112,80},{0,96},{16,112},{3... | collective-permute-start | bytes 356360 | tf_op jit(solution)/shard_map/ppermute | solution.py:33
  15.4 12.9 %collective-permute-start.3 = (bf16[256,928]{1,0:T(8,128)(2,1)S(1)}, bf16[256,928]{1,0:T(8,128)(2,1)S(1)}, u32[]{:S(2)}, u32[]{:S(2)}) collective-permute-start(bf16[256,928]{1,0:T(8,128)(2,1)S(1)} %shard_map.65.rows_ref.after), channel_id=1, source_target_pairs={{0,16},{16,0},{32,48},{48,32},{64,80},{80,64},{96,112},{112,96},{1... | collective-permute-start | bytes 1425416 | tf_op jit(solution)/shard_map/ppermute | solution.py:37
  23.3 20.6 %collective-permute-start.16 = (bf16[256,1664]{1,0:T(8,128)(2,1)S(1)}, bf16[256,1664]{1,0:T(8,128)(2,1)S(1)}, u32[]{:S(2)}, u32[]{:S(2)}) collective-permute-start(bf16[256,1664]{1,0:T(8,128)(2,1)S(1)} %shard_map.66.after), channel_id=1, source_target_pairs={{0,4},{2,6},{1,5},{3,7},{4,0},{6,2},{5,1},{7,3},{8,12},{10,14},{9,... | collective-permute-start | bytes 2555912 | tf_op jit(solution)/shard_map/ppermute | solution.py:28
  26.3 21.5 %collective-permute-start.21 = (bf16[256,1664]{1,0:T(8,128)(2,1)S(1)}, bf16[256,1664]{1,0:T(8,128)(2,1)S(1)}, u32[]{:S(2)}, u32[]{:S(2)}) collective-permute-start(bf16[256,1664]{1,0:T(8,128)(2,1)S(1)} %shard_map.67.after), channel_id=1, source_target_pairs={{0,12},{2,14},{1,13},{3,15},{4,8},{6,10},{5,9},{7,11},{8,4},{10,6}... | collective-permute-start | bytes 2555912 | tf_op jit(solution)/shard_map/ppermute | solution.py:28
  30.0 20.4 %collective-permute-start.4 = (bf16[256,1664]{1,0:T(8,128)(2,1)S(1)}, bf16[256,1664]{1,0:T(8,128)(2,1)S(1)}, u32[]{:S(2)}, u32[]{:S(2)}) collective-permute-start(bf16[256,1664]{1,0:T(8,128)(2,1)S(1)} %shard_map.68.after), channel_id=1, source_target_pairs={{0,2},{2,0},{1,3},{3,1},{4,6},{6,4},{5,7},{7,5},{8,10},{10,8},{9,1... | collective-permute-start | bytes 2555912 | tf_op jit(solution)/shard_map/ppermute | solution.py:28
  33.3 20.9 %collective-permute-start.9 = (bf16[256,1664]{1,0:T(8,128)(2,1)S(1)}, bf16[256,1664]{1,0:T(8,128)(2,1)S(1)}, u32[]{:S(2)}, u32[]{:S(2)}) collective-permute-start(bf16[256,1664]{1,0:T(8,128)(2,1)S(1)} %shard_map.69.after), channel_id=1, source_target_pairs={{0,3},{2,1},{1,2},{3,0},{4,7},{6,5},{5,6},{7,4},{8,11},{10,9},{9,1... | collective-permute-start | bytes 2555912 | tf_op jit(solution)/shard_map/ppermute | solution.py:28
  44.0 13.0 %collective-permute-start.17 = (bf16[128,1664]{1,0:T(8,128)(2,1)S(1)}, bf16[128,1664]{1,0:T(8,128)(2,1)S(1)}, u32[]{:S(2)}, u32[]{:S(2)}) collective-permute-start(bf16[128,1664]{1,0:T(8,128)(2,1)S(1)} %shard_map.89), channel_id=1, source_target_pairs={{0,12},{2,14},{1,13},{3,15},{4,8},{6,10},{5,9},{7,11},{8,4},{10,6}... | collective-permute-start | bytes 1277960 | tf_op jit(solution)/shard_map/ppermute | solution.py:28
  47.9 11.0 %collective-permute-start.22 = (bf16[128,1664]{1,0:T(8,128)(2,1)S(1)}, bf16[128,1664]{1,0:T(8,128)(2,1)S(1)}, u32[]{:S(2)}, u32[]{:S(2)}) collective-permute-start(bf16[128,1664]{1,0:T(8,128)(2,1)S(1)} %shard_map.94), channel_id=1, source_target_pairs={{0,2},{2,0},{1,3},{3,1},{4,6},{6,4},{5,7},{7,5},{8,10},{10,8},{9,1... | collective-permute-start | bytes 1277960 | tf_op jit(solution)/shard_map/ppermute | solution.py:28
  50.4 12.9 %collective-permute-start.5 = (bf16[128,1664]{1,0:T(8,128)(2,1)S(1)}, bf16[128,1664]{1,0:T(8,128)(2,1)S(1)}, u32[]{:S(2)}, u32[]{:S(2)}) collective-permute-start(bf16[128,1664]{1,0:T(8,128)(2,1)S(1)} %shard_map.75), channel_id=1, source_target_pairs={{0,3},{2,1},{1,2},{3,0},{4,7},{6,5},{5,6},{7,4},{8,11},{10,9},{9,1... | collective-permute-start | bytes 1277960 | tf_op jit(solution)/shard_map/ppermute | solution.py:28
  57.2 11.0 %collective-permute-start.18 = (bf16[128,1664]{1,0:T(8,128)(2,1)S(1)}, bf16[128,1664]{1,0:T(8,128)(2,1)S(1)}, u32[]{:S(2)}, u32[]{:S(2)}) collective-permute-start(bf16[128,1664]{1,0:T(8,128)(2,1)S(1)} %get-tuple-element.42), channel_id=1, source_target_pairs={{0,2},{2,0},{1,3},{3,1},{4,6},{6,4},{5,7},{7,5},{8,10},{10,8},{9,1... | collective-permute-start | bytes 1277960 | tf_op jit(solution)/shard_map/ppermute | solution.py:28
  59.0 13.4 %collective-permute-start.23 = (bf16[128,1664]{1,0:T(8,128)(2,1)S(1)}, bf16[128,1664]{1,0:T(8,128)(2,1)S(1)}, u32[]{:S(2)}, u32[]{:S(2)}) collective-permute-start(bf16[128,1664]{1,0:T(8,128)(2,1)S(1)} %get-tuple-element.46), channel_id=1, source_target_pairs={{0,3},{2,1},{1,2},{3,0},{4,7},{6,5},{5,6},{7,4},{8,11},{10,9},{9,1... | collective-permute-start | bytes 1277960 | tf_op jit(solution)/shard_map/ppermute | solution.py:28
  68.3 13.4 %collective-permute-start.19 = (bf16[128,1664]{1,0:T(8,128)(2,1)S(1)}, bf16[128,1664]{1,0:T(8,128)(2,1)S(1)}, u32[]{:S(2)}, u32[]{:S(2)}) collective-permute-start(bf16[128,1664]{1,0:T(8,128)(2,1)S(1)} %get-tuple-element.44), channel_id=1, source_target_pairs={{0,3},{2,1},{1,2},{3,0},{4,7},{6,5},{5,6},{7,4},{8,11},{10,9},{9,1... | collective-permute-start | bytes 1277960 | tf_op jit(solution)/shard_map/ppermute | solution.py:28
  73.3 10.6 %collective-permute-start.7 = (bf16[128,1664]{1,0:T(8,128)(2,1)S(1)}, bf16[128,1664]{1,0:T(8,128)(2,1)S(1)}, u32[]{:S(2)}, u32[]{:S(2)}) collective-permute-start(bf16[128,1664]{1,0:T(8,128)(2,1)S(1)} %get-tuple-element.36), channel_id=1, source_target_pairs={{0,12},{2,14},{1,13},{3,15},{4,8},{6,10},{5,9},{7,11},{8,4},{10,6}... | collective-permute-start | bytes 1277960 | tf_op jit(solution)/shard_map/ppermute | solution.py:28
  74.7 10.8 %collective-permute-start.12 = (bf16[128,1664]{1,0:T(8,128)(2,1)S(1)}, bf16[128,1664]{1,0:T(8,128)(2,1)S(1)}, u32[]{:S(2)}, u32[]{:S(2)}) collective-permute-start(bf16[128,1664]{1,0:T(8,128)(2,1)S(1)} %get-tuple-element.40), channel_id=1, source_target_pairs={{0,2},{2,0},{1,3},{3,1},{4,6},{6,4},{5,7},{7,5},{8,10},{10,8},{9,1... | collective-permute-start | bytes 1277960 | tf_op jit(solution)/shard_map/ppermute | solution.py:28
  82.0 12.5 %collective-permute-start.20 = (bf16[128,1664]{1,0:T(8,128)(2,1)S(1)}, bf16[128,1664]{1,0:T(8,128)(2,1)S(1)}, u32[]{:S(2)}, u32[]{:S(2)}) collective-permute-start(bf16[128,1664]{1,0:T(8,128)(2,1)S(1)} %shard_map.92.refs_0_), channel_id=1, source_target_pairs={{0,12},{2,14},{1,13},{3,15},{4,8},{6,10},{5,9},{7,11},{8,4},{10,6}... | collective-permute-start | bytes 1277960 | tf_op jit(solution)/shard_map/ppermute | solution.py:28
  82.3 12.3 %collective-permute-start.25 = (bf16[128,1664]{1,0:T(8,128)(2,1)S(1)}, bf16[128,1664]{1,0:T(8,128)(2,1)S(1)}, u32[]{:S(2)}, u32[]{:S(2)}) collective-permute-start(bf16[128,1664]{1,0:T(8,128)(2,1)S(1)} %shard_map.97.refs_0_), channel_id=1, source_target_pairs={{0,2},{2,0},{1,3},{3,1},{4,6},{6,4},{5,7},{7,5},{8,10},{10,8},{9,1... | collective-permute-start | bytes 1277960 | tf_op jit(solution)/shard_map/ppermute | solution.py:28
  84.1 11.3 %collective-permute-start.8 = (bf16[128,1664]{1,0:T(8,128)(2,1)S(1)}, bf16[128,1664]{1,0:T(8,128)(2,1)S(1)}, u32[]{:S(2)}, u32[]{:S(2)}) collective-permute-start(bf16[128,1664]{1,0:T(8,128)(2,1)S(1)} %shard_map.78.refs_0_), channel_id=1, source_target_pairs={{0,3},{2,1},{1,2},{3,0},{4,7},{6,5},{5,6},{7,4},{8,11},{10,9},{9,1... | collective-permute-start | bytes 1277960 | tf_op jit(solution)/shard_map/ppermute | solution.py:28
  85.7 10.9 %collective-permute-start.13 = (bf16[128,1664]{1,0:T(8,128)(2,1)S(1)}, bf16[128,1664]{1,0:T(8,128)(2,1)S(1)}, u32[]{:S(2)}, u32[]{:S(2)}) collective-permute-start(bf16[128,1664]{1,0:T(8,128)(2,1)S(1)} %shard_map.83.refs_0_), channel_id=1, source_target_pairs={{0,4},{2,6},{1,5},{3,7},{4,0},{6,2},{5,1},{7,3},{8,12},{10,14},{9,... | collective-permute-start | bytes 1277960 | tf_op jit(solution)/shard_map/ppermute | solution.py:28
  94.5 21.1 %collective-permute-start.26 = (bf16[256,1664]{1,0:T(8,128)(2,1)S(1)}, bf16[256,1664]{1,0:T(8,128)(2,1)S(1)}, u32[]{:S(2)}, u32[]{:S(2)}) collective-permute-start(bf16[256,1664]{1,0:T(8,128)(2,1)S(1)} %shard_map.93.one_ref), channel_id=1, source_target_pairs={{0,4},{2,6},{1,5},{3,7},{4,0},{6,2},{5,1},{7,3},{8,12},{10,14},{9,... | collective-permute-start | bytes 2555912 | tf_op jit(solution)/shard_map/ppermute | solution.py:28
  94.7 22.7 %collective-permute-start.27 = (bf16[256,1664]{1,0:T(8,128)(2,1)S(1)}, bf16[256,1664]{1,0:T(8,128)(2,1)S(1)}, u32[]{:S(2)}, u32[]{:S(2)}) collective-permute-start(bf16[256,1664]{1,0:T(8,128)(2,1)S(1)} %shard_map.98.two_ref), channel_id=1, source_target_pairs={{0,12},{2,14},{1,13},{3,15},{4,8},{6,10},{5,9},{7,11},{8,4},{10,6}... | collective-permute-start | bytes 2555912 | tf_op jit(solution)/shard_map/ppermute | solution.py:28
  95.5 24.1 %collective-permute-start.14 = (bf16[256,1664]{1,0:T(8,128)(2,1)S(1)}, bf16[256,1664]{1,0:T(8,128)(2,1)S(1)}, u32[]{:S(2)}, u32[]{:S(2)}) collective-permute-start(bf16[256,1664]{1,0:T(8,128)(2,1)S(1)} %shard_map.79.one_ref), channel_id=1, source_target_pairs={{0,2},{2,0},{1,3},{3,1},{4,6},{6,4},{5,7},{7,5},{8,10},{10,8},{9,1... | collective-permute-start | bytes 2555912 | tf_op jit(solution)/shard_map/ppermute | solution.py:28
  96.7 24.7 %collective-permute-start.15 = (bf16[256,1664]{1,0:T(8,128)(2,1)S(1)}, bf16[256,1664]{1,0:T(8,128)(2,1)S(1)}, u32[]{:S(2)}, u32[]{:S(2)}) collective-permute-start(bf16[256,1664]{1,0:T(8,128)(2,1)S(1)} %shard_map.84.two_ref), channel_id=1, source_target_pairs={{0,3},{2,1},{1,2},{3,0},{4,7},{6,5},{5,6},{7,4},{8,11},{10,9},{9,1... | collective-permute-start | bytes 2555912 | tf_op jit(solution)/shard_map/ppermute | solution.py:28
  (13 other events, 86.7 us)

commit v2 on v1

--- a/solution.py
+++ b/solution.py
@@ -109,22 +109,25 @@
     return run(pack_kernel, pltpu.VMEM((rows, values[0].shape[1]), BF), *values)
 
 
-def side_bit(ids, side):
-    return (square_bits(ids[1] >> 1) + square_bits(ids[2] * 2 + (ids[1] & 1)))[side % 4]
-
-
-def quarter_of(ids, q, far):
-    return (q % 2) * 2 + (side_bit(ids, q) ^ far)
-
-
-def half_of(ids, q, near, rows):
-    return pl.ds(pl.multiple_of((side_bit(ids, q + 1) ^ near) * rows, rows), rows)
-
-
-def up_kernel(q, far, ids, rows_ref, weight_ref, after, out_ref):
+def side_bit(side):
+    gc = lax.axis_index("gc")
+    if side % 4 < 2:
+        return square_bits(gc >> 1)[side % 4]
+    return square_bits(lax.axis_index("dr") * 2 + (gc & 1))[side % 4 - 2]
+
+
+def quarter_of(q, far):
+    return (q % 2) * 2 + (side_bit(q) ^ far)
+
+
+def half_of(q, near, rows):
+    return pl.ds(pl.multiple_of((side_bit(q + 1) ^ near) * rows, rows), rows)
+
+
+def up_kernel(q, far, rows_ref, weight_ref, after, out_ref):
     half = out_ref.shape[0] // 2
-    rows = jnp.concatenate([rows_ref[half_of(ids, q, near, half)] for near in range(2)])
-    quarter = quarter_of(ids, q, far)
+    rows = jnp.concatenate([rows_ref[half_of(q, near, half)] for near in range(2)])
+    quarter = quarter_of(q, far)
     width = weight_ref.shape[2]
     for start in range(0, width, 256):
         stop = min(start + 256, width)
@@ -156,30 +159,30 @@
     out_ref[...] = value.astype(BF)
 
 
-def add_down(ids, q, far, rows_ref, weight_ref, from_ref, out_ref):
+def add_down(q, far, rows_ref, weight_ref, from_ref, out_ref):
     half = out_ref.shape[0] // 2
     value = lax.dot_general(
         rows_ref[...],
-        weight_ref[quarter_of(ids, q, far)],
+        weight_ref[quarter_of(q, far)],
         (((1,), (1,)), ((), ())),
         preferred_element_type=F32,
     )
     for near in range(2):
-        at = half_of(ids, q, near, half)
+        at = half_of(q, near, half)
         rows = value[near * half : (near + 1) * half]
         out_ref[at] = rows if from_ref is None else from_ref[at] + rows
 
 
-def down_own_kernel(q, ids, one_ref, two_ref, weight_ref, out_ref):
-    add_down(ids, q, 0, one_ref, weight_ref, None, out_ref)
-    add_down(ids, q + 1, 0, two_ref, weight_ref, out_ref, out_ref)
-
-
-def down_kernel(q, ids, total_ref, rows_ref, weight_ref, out_ref):
-    add_down(ids, q, 1, rows_ref, weight_ref, total_ref, out_ref)
-
-
-def index_kernel(ids, sizes_ref, map_ref, order_ref, after, out_ref, mid_ref):
+def down_own_kernel(q, one_ref, two_ref, weight_ref, out_ref):
+    add_down(q, 0, one_ref, weight_ref, None, out_ref)
+    add_down(q + 1, 0, two_ref, weight_ref, out_ref, out_ref)
+
+
+def down_kernel(q, total_ref, rows_ref, weight_ref, out_ref):
+    add_down(q, 1, rows_ref, weight_ref, total_ref, out_ref)
+
+
+def index_kernel(sizes_ref, map_ref, order_ref, after, out_ref, mid_ref):
     rows = order_ref.shape[1]
     reqs = sizes_ref.shape[1]
     own = rows // 8
@@ -198,7 +201,8 @@
     order = order_ref[...]
     inside = (order >= start) & (order < start + upright(sizes))
     source = order + jnp.sum(jnp.where(inside, shift, 0), axis=0, keepdims=True)
-    chip, core = ids[0] >> 1, ids[0] & 1
+    g = lax.axis_index("gr")
+    chip, core = g >> 1, g & 1
     ahead = (source // (2 * own) - chip) & 3
     slot = jnp.where(ahead == 2, 1, jnp.where(ahead == 1, 2, ahead))
     at = (((source // own) & 1) ^ core) * (4 * own) + slot * own + source % own
@@ -247,9 +251,6 @@
     part = hidden_units // 4
     group = rows // 2
     chains = range(4)
-    ids = jnp.stack([lax.axis_index("gr"), lax.axis_index("gc"), lax.axis_index("dr")])
-    ids = ids.astype(jnp.int32)
-    smem = pltpu.SMEM
 
     fetched = [from_chip(draft_rows, ahead) for ahead in (2, 1, 3)]
     ups, draft = load(up_weight, draft_rows)
@@ -262,11 +263,10 @@
         return run(
             functools.partial(up_kernel, q, far),
             pltpu.VMEM((group, part), dtype),
-            ids,
             column if q < 2 else beside,
             ups,
             after,
-            spaces={0: smem, 3: pl.ANY},
+            spaces={2: pl.ANY},
             flops=project_flops,
         )
 
@@ -282,12 +282,11 @@
     pick = run(
         index_kernel,
         pltpu.VMEM((rows, rows), BF),
-        ids,
         tree_sizes[None, :],
         draft_map[None, :],
         row_order[None, :],
         after,
-        spaces={0: smem, 4: pl.ANY},
+        spaces={3: pl.ANY},
         flops=rows * rows * 64,
         scratch=[pltpu.VMEM((rows, rows), BF)],
     )
@@ -314,23 +313,19 @@
         total = run(
             functools.partial(down_own_kernel, 2 * i),
             whole,
-            ids,
             mine[2 * i],
             mine[2 * i + 1],
             downs,
-            spaces={0: smem},
             flops=2 * project_flops,
         )
         for q in (2 * i, 2 * i + 1):
             total = run(
                 functools.partial(down_kernel, q),
                 whole,
-                ids,
-                total,
+                    total,
                 came[q],
                 downs,
-                spaces={0: smem},
-                flops=project_flops,
+                    flops=project_flops,
             )
         sorted_rows = run(
             functools.partial(sort_kernel, i * group),

time: 138 us -> 124 us (0.90)
  local copies, waits for them, and re-layouts: 8.95 us -> 0.01 us
  Pallas kernels: 40.5 us -> 32.2 us
  starting transfers between devices: 46.2 us -> 48.4 us
    unnamed x10 -> x6, local copies, waits for them, and re-layouts: 8.95 us -> 0.01 us
    pallas_call x42, Pallas kernels: 40.5 us -> 32.2 us  [run(): pl.pallas_call(kernel, out_shape=shapes, in_specs=specs, out_specs=[vmem]...]
    ppermute x24, waiting for transfers between devices: 32.4 us -> 34.7 us  [swap(): return lax.ppermute(value, YZ, SWAPS[side])]
    ppermute x24, starting transfers between devices: 34.5 us -> 36.1 us  [swap(): return lax.ppermute(value, YZ, SWAPS[side])]
  transfers between devices with their start and end apart: 32 -> 32, of which waited for: 17 -> 14; matrix products, arithmetic and copies ran while one was open for 0% -> 0% of each run, Pallas kernels for 27% -> 24%
where the time goes in v2:
time: 124 us
  starting transfers between devices  48.4 us (39%)
  waiting for transfers between devices  42.9 us (35%)
  Pallas kernels  32.2 us (26%)
    ppermute x24, starting transfers between devices, swap(): return lax.ppermute(value, YZ, SWAPS[side])  36.1 us
    ppermute x24, waiting for transfers between devices, swap(): return lax.ppermute(value, YZ, SWAPS[side])  34.7 us
    pallas_call x42, Pallas kernels, run(): pl.pallas_call(kernel, out_shape=shapes, in_specs=specs, out_specs=[vmem]...  32.2 us
    ppermute x6, starting transfers between devices, from_chip(): return lax.ppermute(value, 'gr', pairs)  8.82 us
    ppermute x6, waiting for transfers between devices, from_chip(): return lax.ppermute(value, 'gr', pairs)  6.68 us
    ppermute x2, starting transfers between devices, other_core(): return lax.ppermute(value, 'gr', [(i, i ^ 1) for i in range(8)])  3.46 us
  transfers between devices with their start and end apart: 32, of which 14 were waited for; matrix products, arithmetic and copies ran while one was open for 0% of the time, Pallas kernels for 24%

profile of v2, /device:TPU:1, one launch (start us, length us, event | category | flops | bytes accessed | tf_op | source)
XLA Modules:
  0.0 123.9 jit_solution(13721638609274630530)
XLA Ops:
  0.0 3.6 %collective-permute-start = (bf16[64,928]{1,0:T(8,128)(2,1)}, bf16[64,928]{1,0:T(8,128)(2,1)S(1)}, u32[]{:S(2)}, u32[]{:S(2)}) collective-permute-start(bf16[64,928]{1,0:T(8,128)(2,1)} %refs_1_.1), channel_id=1, source_target_pairs={{64,0},{80,16},{96,32},{112,48},{0,64},{16,80},{32,96},{48,112},{6... | collective-permute-start | bytes 356360 | tf_op jit(solution)/shard_map/ppermute | solution.py:33
  3.9 2.4 %collective-permute-start.1 = (bf16[64,928]{1,0:T(8,128)(2,1)}, bf16[64,928]{1,0:T(8,128)(2,1)S(1)}, u32[]{:S(2)}, u32[]{:S(2)}) collective-permute-start(bf16[64,928]{1,0:T(8,128)(2,1)} %refs_1_.1), channel_id=1, source_target_pairs={{32,0},{48,16},{64,32},{80,48},{96,64},{112,80},{0,96},{16,112},{3... | collective-permute-start | bytes 356360 | tf_op jit(solution)/shard_map/ppermute | solution.py:33
  6.3 4.7 %shard_map.64 = (bf16[4,928,1664]{2,1,0:T(8,128)(2,1)S(1)}, bf16[64,928]{1,0:T(8,128)(2,1)S(1)}) custom-call(bf16[928,6656]{1,0:T(8,128)(2,1)} %refs_0_.1, bf16[64,928]{1,0:T(8,128)(2,1)} %refs_1_.1), custom_call_target="tpu_custom_call" | custom-call | bytes 24707072 | tf_op jit(solution)/shard_map/pallas_call | solution.py:52
  16.2 2.0 %collective-permute-start.21 = (bf16[256,1664]{1,0:T(8,128)(2,1)S(1)}, bf16[256,1664]{1,0:T(8,128)(2,1)S(1)}, u32[]{:S(2)}, u32[]{:S(2)}) collective-permute-start(bf16[256,1664]{1,0:T(8,128)(2,1)S(1)} %shard_map.67.after), channel_id=1, source_target_pairs={{0,12},{2,14},{1,13},{3,15},{4,8},{6,10},{5,9},{7,11},{8,4},{10,6}... | collective-permute-start | bytes 2555912 | tf_op jit(solution)/shard_map/ppermute | solution.py:28
  22.2 2.3 %collective-permute-start.9 = (bf16[256,1664]{1,0:T(8,128)(2,1)S(1)}, bf16[256,1664]{1,0:T(8,128)(2,1)S(1)}, u32[]{:S(2)}, u32[]{:S(2)}) collective-permute-start(bf16[256,1664]{1,0:T(8,128)(2,1)S(1)} %shard_map.69.after), channel_id=1, source_target_pairs={{0,3},{2,1},{1,2},{3,0},{4,7},{6,5},{5,6},{7,4},{8,11},{10,9},{9,1... | collective-permute-start | bytes 2555912 | tf_op jit(solution)/shard_map/ppermute | solution.py:28
  29.0 5.4 %collective-permute-done.16.got_ref = bf16[256,1664]{1,0:T(8,128)(2,1)S(1)} collective-permute-done((bf16[256,1664]{1,0:T(8,128)(2,1)S(1)}, bf16[256,1664]{1,0:T(8,128)(2,1)S(1)}, u32[]{:S(2)}, u32[]{:S(2)}) %collective-permute-start.16) | collective-permute-done | bytes 852000 | tf_op jit(solution)/shard_map/ppermute | solution.py:28
  34.4 2.8 %collective-permute-start.17 = (bf16[128,1664]{1,0:T(8,128)(2,1)S(1)}, bf16[128,1664]{1,0:T(8,128)(2,1)S(1)}, u32[]{:S(2)}, u32[]{:S(2)}) collective-permute-start(bf16[128,1664]{1,0:T(8,128)(2,1)S(1)} %shard_map.89), channel_id=1, source_target_pairs={{0,12},{2,14},{1,13},{3,15},{4,8},{6,10},{5,9},{7,11},{8,4},{10,6}... | collective-permute-start | bytes 1277960 | tf_op jit(solution)/shard_map/ppermute | solution.py:28
  39.7 3.5 %collective-permute-start.5 = (bf16[128,1664]{1,0:T(8,128)(2,1)S(1)}, bf16[128,1664]{1,0:T(8,128)(2,1)S(1)}, u32[]{:S(2)}, u32[]{:S(2)}) collective-permute-start(bf16[128,1664]{1,0:T(8,128)(2,1)S(1)} %shard_map.75), channel_id=1, source_target_pairs={{0,3},{2,1},{1,2},{3,0},{4,7},{6,5},{5,6},{7,4},{8,11},{10,9},{9,1... | collective-permute-start | bytes 1277960 | tf_op jit(solution)/shard_map/ppermute | solution.py:28
  43.8 2.6 %collective-permute-done.17.new_ref = bf16[128,1664]{1,0:T(8,128)(2,1)S(1)} collective-permute-done((bf16[128,1664]{1,0:T(8,128)(2,1)S(1)}, bf16[128,1664]{1,0:T(8,128)(2,1)S(1)}, u32[]{:S(2)}, u32[]{:S(2)}) %collective-permute-start.17) | collective-permute-done | bytes 426016 | tf_op jit(solution)/shard_map/ppermute | solution.py:28
  46.5 1.7 %collective-permute-start.18 = (bf16[128,1664]{1,0:T(8,128)(2,1)S(1)}, bf16[128,1664]{1,0:T(8,128)(2,1)S(1)}, u32[]{:S(2)}, u32[]{:S(2)}) collective-permute-start(bf16[128,1664]{1,0:T(8,128)(2,1)S(1)} %get-tuple-element.42), channel_id=1, source_target_pairs={{0,2},{2,0},{1,3},{3,1},{4,6},{6,4},{5,7},{7,5},{8,10},{10,8},{9,1... | collective-permute-start | bytes 1277960 | tf_op jit(solution)/shard_map/ppermute | solution.py:28
  48.5 3.5 %collective-permute-start.23 = (bf16[128,1664]{1,0:T(8,128)(2,1)S(1)}, bf16[128,1664]{1,0:T(8,128)(2,1)S(1)}, u32[]{:S(2)}, u32[]{:S(2)}) collective-permute-start(bf16[128,1664]{1,0:T(8,128)(2,1)S(1)} %get-tuple-element.46), channel_id=1, source_target_pairs={{0,3},{2,1},{1,2},{3,0},{4,7},{6,5},{5,6},{7,4},{8,11},{10,9},{9,1... | collective-permute-start | bytes 1277960 | tf_op jit(solution)/shard_map/ppermute | solution.py:28
  54.6 2.8 %collective-permute-done.18.got_ref = bf16[128,1664]{1,0:T(8,128)(2,1)S(1)} collective-permute-done((bf16[128,1664]{1,0:T(8,128)(2,1)S(1)}, bf16[128,1664]{1,0:T(8,128)(2,1)S(1)}, u32[]{:S(2)}, u32[]{:S(2)}) %collective-permute-start.18) | collective-permute-done | bytes 426016 | tf_op jit(solution)/shard_map/ppermute | solution.py:28
  57.5 3.5 %collective-permute-start.19 = (bf16[128,1664]{1,0:T(8,128)(2,1)S(1)}, bf16[128,1664]{1,0:T(8,128)(2,1)S(1)}, u32[]{:S(2)}, u32[]{:S(2)}) collective-permute-start(bf16[128,1664]{1,0:T(8,128)(2,1)S(1)} %get-tuple-element.44), channel_id=1, source_target_pairs={{0,3},{2,1},{1,2},{3,0},{4,7},{6,5},{5,6},{7,4},{8,11},{10,9},{9,1... | collective-permute-start | bytes 1277960 | tf_op jit(solution)/shard_map/ppermute | solution.py:28
  63.8 6.1 %collective-permute-done.19.got_ref = bf16[128,1664]{1,0:T(8,128)(2,1)S(1)} collective-permute-done((bf16[128,1664]{1,0:T(8,128)(2,1)S(1)}, bf16[128,1664]{1,0:T(8,128)(2,1)S(1)}, u32[]{:S(2)}, u32[]{:S(2)}) %collective-permute-start.19) | collective-permute-done | bytes 426016 | tf_op jit(solution)/shard_map/ppermute | solution.py:28
  74.6 8.7 %collective-permute-done.20.refs_1_ = bf16[128,1664]{1,0:T(8,128)(2,1)S(1)} collective-permute-done((bf16[128,1664]{1,0:T(8,128)(2,1)S(1)}, bf16[128,1664]{1,0:T(8,128)(2,1)S(1)}, u32[]{:S(2)}, u32[]{:S(2)}) %collective-permute-start.20) | collective-permute-done | bytes 426016 | tf_op jit(solution)/shard_map/ppermute | solution.py:28
  84.8 2.1 %collective-permute-start.15 = (bf16[256,1664]{1,0:T(8,128)(2,1)S(1)}, bf16[256,1664]{1,0:T(8,128)(2,1)S(1)}, u32[]{:S(2)}, u32[]{:S(2)}) collective-permute-start(bf16[256,1664]{1,0:T(8,128)(2,1)S(1)} %shard_map.84.two_ref), channel_id=1, source_target_pairs={{0,3},{2,1},{1,2},{3,0},{4,7},{6,5},{5,6},{7,4},{8,11},{10,9},{9,1... | collective-permute-start | bytes 2555912 | tf_op jit(solution)/shard_map/ppermute | solution.py:28
  86.9 4.7 %shard_map.85.weight_ref = bf16[4,928,1664]{2,1,0:T(8,128)(2,1)S(1)} custom-call(bf16[928,6656]{1,0:T(8,128)(2,1)} %bitcast.7, f32[256,1664]{1,0:T(8,128)S(1)} %shard_map.73.after.kept_ref.refs_1_), custom_call_target="tpu_custom_call" | custom-call | bytes 24707072 | tf_op jit(solution)/shard_map/pallas_call | solution.py:52
  92.2 2.1 %shard_map.99.total_ref = f32[256,928]{1,0:T(8,128)S(1)} custom-call(bf16[256,1664]{1,0:T(8,128)(2,1)S(1)} %shard_map.93.one_ref, bf16[256,1664]{1,0:T(8,128)(2,1)S(1)} %shard_map.98.two_ref, bf16[4,928,1664]{2,1,0:T(8,128)(2,1)S(1)} %shard_map.85.weight_ref), custom_call_target="tpu_custom_call" | custom-call | flops 1581252608 | bytes 14057472 | tf_op jit(solution)/shard_map/pallas_call | solution.py:52
  94.3 2.1 %shard_map.86.total_ref = f32[256,928]{1,0:T(8,128)S(1)} custom-call(bf16[256,1664]{1,0:T(8,128)(2,1)S(1)} %shard_map.79.one_ref, bf16[256,1664]{1,0:T(8,128)(2,1)S(1)} %shard_map.84.two_ref, bf16[4,928,1664]{2,1,0:T(8,128)(2,1)S(1)} %shard_map.85.weight_ref), custom_call_target="tpu_custom_call" | custom-call | flops 1581252608 | bytes 14057472 | tf_op jit(solution)/shard_map/pallas_call | solution.py:52
  96.4 8.1 %collective-permute-done.26.rows_ref = bf16[256,1664]{1,0:T(8,128)(2,1)S(1)} collective-permute-done((bf16[256,1664]{1,0:T(8,128)(2,1)S(1)}, bf16[256,1664]{1,0:T(8,128)(2,1)S(1)}, u32[]{:S(2)}, u32[]{:S(2)}) %collective-permute-start.26) | collective-permute-done | bytes 852000 | tf_op jit(solution)/shard_map/ppermute | solution.py:28
  110.4 1.9 %collective-permute-start.28 = (bf16[256,928]{1,0:T(8,128)(2,1)S(1)}, bf16[256,928]{1,0:T(8,128)(2,1)S(1)}, u32[]{:S(2)}, u32[]{:S(2)}) collective-permute-start(bf16[256,928]{1,0:T(8,128)(2,1)S(1)} %get-tuple-element.52), channel_id=1, source_target_pairs={{0,16},{16,0},{32,48},{48,32},{64,80},{80,64},{96,112},{112,96},{1... | collective-permute-start | bytes 1425416 | tf_op jit(solution)/shard_map/ppermute | solution.py:37
  114.7 1.8 %collective-permute-start.30 = (bf16[64,928]{1,0:T(8,128)(2,1)S(1)}, bf16[64,928]{1,0:T(8,128)(2,1)S(1)}, u32[]{:S(2)}, u32[]{:S(2)}) collective-permute-start(bf16[64,928]{1,0:T(8,128)(2,1)S(1)} %get-tuple-element.55), channel_id=1, source_target_pairs={{32,0},{48,16},{64,32},{80,48},{96,64},{112,80},{0,96},{16,112},{3... | collective-permute-start | bytes 356360 | tf_op jit(solution)/shard_map/ppermute | solution.py:33
  116.5 3.7 %collective-permute-done.29.refs_0_ = bf16[64,928]{1,0:T(8,128)(2,1)S(1)} collective-permute-done((bf16[64,928]{1,0:T(8,128)(2,1)S(1)}, bf16[64,928]{1,0:T(8,128)(2,1)S(1)}, u32[]{:S(2)}, u32[]{:S(2)}) %collective-permute-start.29) | collective-permute-done | bytes 118816 | tf_op jit(solution)/shard_map/ppermute | solution.py:33
  120.2 2.2 %collective-permute-done.30.refs_1_ = bf16[64,928]{1,0:T(8,128)(2,1)S(1)} collective-permute-done((bf16[64,928]{1,0:T(8,128)(2,1)S(1)}, bf16[64,928]{1,0:T(8,128)(2,1)S(1)}, u32[]{:S(2)}, u32[]{:S(2)}) %collective-permute-start.30) | collective-permute-done | bytes 118816 | tf_op jit(solution)/shard_map/ppermute | solution.py:33
  (88 shorter events, 39.6 us)
Async XLA Ops:
  0.0 10.9 %collective-permute-start = (bf16[64,928]{1,0:T(8,128)(2,1)}, bf16[64,928]{1,0:T(8,128)(2,1)S(1)}, u32[]{:S(2)}, u32[]{:S(2)}) collective-permute-start(bf16[64,928]{1,0:T(8,128)(2,1)} %refs_1_.1), channel_id=1, source_target_pairs={{64,0},{80,16},{96,32},{112,48},{0,64},{16,80},{32,96},{48,112},{6... | collective-permute-start | bytes 356360 | tf_op jit(solution)/shard_map/ppermute | solution.py:33
  13.7 20.6 %collective-permute-start.16 = (bf16[256,1664]{1,0:T(8,128)(2,1)S(1)}, bf16[256,1664]{1,0:T(8,128)(2,1)S(1)}, u32[]{:S(2)}, u32[]{:S(2)}) collective-permute-start(bf16[256,1664]{1,0:T(8,128)(2,1)S(1)} %shard_map.66.after), channel_id=1, source_target_pairs={{0,4},{2,6},{1,5},{3,7},{4,0},{6,2},{5,1},{7,3},{8,12},{10,14},{9,... | collective-permute-start | bytes 2555912 | tf_op jit(solution)/shard_map/ppermute | solution.py:28
  16.2 21.5 %collective-permute-start.21 = (bf16[256,1664]{1,0:T(8,128)(2,1)S(1)}, bf16[256,1664]{1,0:T(8,128)(2,1)S(1)}, u32[]{:S(2)}, u32[]{:S(2)}) collective-permute-start(bf16[256,1664]{1,0:T(8,128)(2,1)S(1)} %shard_map.67.after), channel_id=1, source_target_pairs={{0,12},{2,14},{1,13},{3,15},{4,8},{6,10},{5,9},{7,11},{8,4},{10,6}... | collective-permute-start | bytes 2555912 | tf_op jit(solution)/shard_map/ppermute | solution.py:28
  19.3 20.4 %collective-permute-start.4 = (bf16[256,1664]{1,0:T(8,128)(2,1)S(1)}, bf16[256,1664]{1,0:T(8,128)(2,1)S(1)}, u32[]{:S(2)}, u32[]{:S(2)}) collective-permute-start(bf16[256,1664]{1,0:T(8,128)(2,1)S(1)} %shard_map.68.after), channel_id=1, source_target_pairs={{0,2},{2,0},{1,3},{3,1},{4,6},{6,4},{5,7},{7,5},{8,10},{10,8},{9,1... | collective-permute-start | bytes 2555912 | tf_op jit(solution)/shard_map/ppermute | solution.py:28
  22.2 21.0 %collective-permute-start.9 = (bf16[256,1664]{1,0:T(8,128)(2,1)S(1)}, bf16[256,1664]{1,0:T(8,128)(2,1)S(1)}, u32[]{:S(2)}, u32[]{:S(2)}) collective-permute-start(bf16[256,1664]{1,0:T(8,128)(2,1)S(1)} %shard_map.69.after), channel_id=1, source_target_pairs={{0,3},{2,1},{1,2},{3,0},{4,7},{6,5},{5,6},{7,4},{8,11},{10,9},{9,1... | collective-permute-start | bytes 2555912 | tf_op jit(solution)/shard_map/ppermute | solution.py:28
  34.4 11.9 %collective-permute-start.17 = (bf16[128,1664]{1,0:T(8,128)(2,1)S(1)}, bf16[128,1664]{1,0:T(8,128)(2,1)S(1)}, u32[]{:S(2)}, u32[]{:S(2)}) collective-permute-start(bf16[128,1664]{1,0:T(8,128)(2,1)S(1)} %shard_map.89), channel_id=1, source_target_pairs={{0,12},{2,14},{1,13},{3,15},{4,8},{6,10},{5,9},{7,11},{8,4},{10,6}... | collective-permute-start | bytes 1277960 | tf_op jit(solution)/shard_map/ppermute | solution.py:28
  37.8 10.6 %collective-permute-start.22 = (bf16[128,1664]{1,0:T(8,128)(2,1)S(1)}, bf16[128,1664]{1,0:T(8,128)(2,1)S(1)}, u32[]{:S(2)}, u32[]{:S(2)}) collective-permute-start(bf16[128,1664]{1,0:T(8,128)(2,1)S(1)} %shard_map.94), channel_id=1, source_target_pairs={{0,2},{2,0},{1,3},{3,1},{4,6},{6,4},{5,7},{7,5},{8,10},{10,8},{9,1... | collective-permute-start | bytes 1277960 | tf_op jit(solution)/shard_map/ppermute | solution.py:28
  39.7 12.3 %collective-permute-start.5 = (bf16[128,1664]{1,0:T(8,128)(2,1)S(1)}, bf16[128,1664]{1,0:T(8,128)(2,1)S(1)}, u32[]{:S(2)}, u32[]{:S(2)}) collective-permute-start(bf16[128,1664]{1,0:T(8,128)(2,1)S(1)} %shard_map.75), channel_id=1, source_target_pairs={{0,3},{2,1},{1,2},{3,0},{4,7},{6,5},{5,6},{7,4},{8,11},{10,9},{9,1... | collective-permute-start | bytes 1277960 | tf_op jit(solution)/shard_map/ppermute | solution.py:28
  43.3 9.8 %collective-permute-start.10 = (bf16[128,1664]{1,0:T(8,128)(2,1)S(1)}, bf16[128,1664]{1,0:T(8,128)(2,1)S(1)}, u32[]{:S(2)}, u32[]{:S(2)}) collective-permute-start(bf16[128,1664]{1,0:T(8,128)(2,1)S(1)} %shard_map.80), channel_id=1, source_target_pairs={{0,4},{2,6},{1,5},{3,7},{4,0},{6,2},{5,1},{7,3},{8,12},{10,14},{9,... | collective-permute-start | bytes 1277960 | tf_op jit(solution)/shard_map/ppermute | solution.py:28
  46.5 10.9 %collective-permute-start.18 = (bf16[128,1664]{1,0:T(8,128)(2,1)S(1)}, bf16[128,1664]{1,0:T(8,128)(2,1)S(1)}, u32[]{:S(2)}, u32[]{:S(2)}) collective-permute-start(bf16[128,1664]{1,0:T(8,128)(2,1)S(1)} %get-tuple-element.42), channel_id=1, source_target_pairs={{0,2},{2,0},{1,3},{3,1},{4,6},{6,4},{5,7},{7,5},{8,10},{10,8},{9,1... | collective-permute-start | bytes 1277960 | tf_op jit(solution)/shard_map/ppermute | solution.py:28
  48.5 12.5 %collective-permute-start.23 = (bf16[128,1664]{1,0:T(8,128)(2,1)S(1)}, bf16[128,1664]{1,0:T(8,128)(2,1)S(1)}, u32[]{:S(2)}, u32[]{:S(2)}) collective-permute-start(bf16[128,1664]{1,0:T(8,128)(2,1)S(1)} %get-tuple-element.46), channel_id=1, source_target_pairs={{0,3},{2,1},{1,2},{3,0},{4,7},{6,5},{5,6},{7,4},{8,11},{10,9},{9,1... | collective-permute-start | bytes 1277960 | tf_op jit(solution)/shard_map/ppermute | solution.py:28
  53.2 10.2 %collective-permute-start.11 = (bf16[128,1664]{1,0:T(8,128)(2,1)S(1)}, bf16[128,1664]{1,0:T(8,128)(2,1)S(1)}, u32[]{:S(2)}, u32[]{:S(2)}) collective-permute-start(bf16[128,1664]{1,0:T(8,128)(2,1)S(1)} %get-tuple-element.38), channel_id=1, source_target_pairs={{0,12},{2,14},{1,13},{3,15},{4,8},{6,10},{5,9},{7,11},{8,4},{10,6}... | collective-permute-start | bytes 1277960 | tf_op jit(solution)/shard_map/ppermute | solution.py:28
  57.5 12.3 %collective-permute-start.19 = (bf16[128,1664]{1,0:T(8,128)(2,1)S(1)}, bf16[128,1664]{1,0:T(8,128)(2,1)S(1)}, u32[]{:S(2)}, u32[]{:S(2)}) collective-permute-start(bf16[128,1664]{1,0:T(8,128)(2,1)S(1)} %get-tuple-element.44), channel_id=1, source_target_pairs={{0,3},{2,1},{1,2},{3,0},{4,7},{6,5},{5,6},{7,4},{8,11},{10,9},{9,1... | collective-permute-start | bytes 1277960 | tf_op jit(solution)/shard_map/ppermute | solution.py:28
  61.1 10.1 %collective-permute-start.24 = (bf16[128,1664]{1,0:T(8,128)(2,1)S(1)}, bf16[128,1664]{1,0:T(8,128)(2,1)S(1)}, u32[]{:S(2)}, u32[]{:S(2)}) collective-permute-start(bf16[128,1664]{1,0:T(8,128)(2,1)S(1)} %get-tuple-element.48), channel_id=1, source_target_pairs={{0,4},{2,6},{1,5},{3,7},{4,0},{6,2},{5,1},{7,3},{8,12},{10,14},{9,... | collective-permute-start | bytes 1277960 | tf_op jit(solution)/shard_map/ppermute | solution.py:28
  61.7 10.7 %collective-permute-start.7 = (bf16[128,1664]{1,0:T(8,128)(2,1)S(1)}, bf16[128,1664]{1,0:T(8,128)(2,1)S(1)}, u32[]{:S(2)}, u32[]{:S(2)}) collective-permute-start(bf16[128,1664]{1,0:T(8,128)(2,1)S(1)} %get-tuple-element.36), channel_id=1, source_target_pairs={{0,12},{2,14},{1,13},{3,15},{4,8},{6,10},{5,9},{7,11},{8,4},{10,6}... | collective-permute-start | bytes 1277960 | tf_op jit(solution)/shard_map/ppermute | solution.py:28
  63.5 10.8 %collective-permute-start.12 = (bf16[128,1664]{1,0:T(8,128)(2,1)S(1)}, bf16[128,1664]{1,0:T(8,128)(2,1)S(1)}, u32[]{:S(2)}, u32[]{:S(2)}) collective-permute-start(bf16[128,1664]{1,0:T(8,128)(2,1)S(1)} %get-tuple-element.40), channel_id=1, source_target_pairs={{0,2},{2,0},{1,3},{3,1},{4,6},{6,4},{5,7},{7,5},{8,10},{10,8},{9,1... | collective-permute-start | bytes 1277960 | tf_op jit(solution)/shard_map/ppermute | solution.py:28
  70.1 13.2 %collective-permute-start.20 = (bf16[128,1664]{1,0:T(8,128)(2,1)S(1)}, bf16[128,1664]{1,0:T(8,128)(2,1)S(1)}, u32[]{:S(2)}, u32[]{:S(2)}) collective-permute-start(bf16[128,1664]{1,0:T(8,128)(2,1)S(1)} %shard_map.92.refs_0_), channel_id=1, source_target_pairs={{0,12},{2,14},{1,13},{3,15},{4,8},{6,10},{5,9},{7,11},{8,4},{10,6}... | collective-permute-start | bytes 1277960 | tf_op jit(solution)/shard_map/ppermute | solution.py:28
  71.4 12.0 %collective-permute-start.25 = (bf16[128,1664]{1,0:T(8,128)(2,1)S(1)}, bf16[128,1664]{1,0:T(8,128)(2,1)S(1)}, u32[]{:S(2)}, u32[]{:S(2)}) collective-permute-start(bf16[128,1664]{1,0:T(8,128)(2,1)S(1)} %shard_map.97.refs_0_), channel_id=1, source_target_pairs={{0,2},{2,0},{1,3},{3,1},{4,6},{6,4},{5,7},{7,5},{8,10},{10,8},{9,1... | collective-permute-start | bytes 1277960 | tf_op jit(solution)/shard_map/ppermute | solution.py:28
  72.6 11.8 %collective-permute-start.8 = (bf16[128,1664]{1,0:T(8,128)(2,1)S(1)}, bf16[128,1664]{1,0:T(8,128)(2,1)S(1)}, u32[]{:S(2)}, u32[]{:S(2)}) collective-permute-start(bf16[128,1664]{1,0:T(8,128)(2,1)S(1)} %shard_map.78.refs_0_), channel_id=1, source_target_pairs={{0,3},{2,1},{1,2},{3,0},{4,7},{6,5},{5,6},{7,4},{8,11},{10,9},{9,1... | collective-permute-start | bytes 1277960 | tf_op jit(solution)/shard_map/ppermute | solution.py:28
  74.6 10.2 %collective-permute-start.13 = (bf16[128,1664]{1,0:T(8,128)(2,1)S(1)}, bf16[128,1664]{1,0:T(8,128)(2,1)S(1)}, u32[]{:S(2)}, u32[]{:S(2)}) collective-permute-start(bf16[128,1664]{1,0:T(8,128)(2,1)S(1)} %shard_map.83.refs_0_), channel_id=1, source_target_pairs={{0,4},{2,6},{1,5},{3,7},{4,0},{6,2},{5,1},{7,3},{8,12},{10,14},{9,... | collective-permute-start | bytes 1277960 | tf_op jit(solution)/shard_map/ppermute | solution.py:28
  83.4 21.1 %collective-permute-start.26 = (bf16[256,1664]{1,0:T(8,128)(2,1)S(1)}, bf16[256,1664]{1,0:T(8,128)(2,1)S(1)}, u32[]{:S(2)}, u32[]{:S(2)}) collective-permute-start(bf16[256,1664]{1,0:T(8,128)(2,1)S(1)} %shard_map.93.one_ref), channel_id=1, source_target_pairs={{0,4},{2,6},{1,5},{3,7},{4,0},{6,2},{5,1},{7,3},{8,12},{10,14},{9,... | collective-permute-start | bytes 2555912 | tf_op jit(solution)/shard_map/ppermute | solution.py:28
  83.5 22.1 %collective-permute-start.27 = (bf16[256,1664]{1,0:T(8,128)(2,1)S(1)}, bf16[256,1664]{1,0:T(8,128)(2,1)S(1)}, u32[]{:S(2)}, u32[]{:S(2)}) collective-permute-start(bf16[256,1664]{1,0:T(8,128)(2,1)S(1)} %shard_map.98.two_ref), channel_id=1, source_target_pairs={{0,12},{2,14},{1,13},{3,15},{4,8},{6,10},{5,9},{7,11},{8,4},{10,6}... | collective-permute-start | bytes 2555912 | tf_op jit(solution)/shard_map/ppermute | solution.py:28
  84.5 22.9 %collective-permute-start.14 = (bf16[256,1664]{1,0:T(8,128)(2,1)S(1)}, bf16[256,1664]{1,0:T(8,128)(2,1)S(1)}, u32[]{:S(2)}, u32[]{:S(2)}) collective-permute-start(bf16[256,1664]{1,0:T(8,128)(2,1)S(1)} %shard_map.79.one_ref), channel_id=1, source_target_pairs={{0,2},{2,0},{1,3},{3,1},{4,6},{6,4},{5,7},{7,5},{8,10},{10,8},{9,1... | collective-permute-start | bytes 2555912 | tf_op jit(solution)/shard_map/ppermute | solution.py:28
  84.8 23.8 %collective-permute-start.15 = (bf16[256,1664]{1,0:T(8,128)(2,1)S(1)}, bf16[256,1664]{1,0:T(8,128)(2,1)S(1)}, u32[]{:S(2)}, u32[]{:S(2)}) collective-permute-start(bf16[256,1664]{1,0:T(8,128)(2,1)S(1)} %shard_map.84.two_ref), channel_id=1, source_target_pairs={{0,3},{2,1},{1,2},{3,0},{4,7},{6,5},{5,6},{7,4},{8,11},{10,9},{9,1... | collective-permute-start | bytes 2555912 | tf_op jit(solution)/shard_map/ppermute | solution.py:28
  (11 other events, 69.1 us)

commit v3 on v2

--- a/solution.py
+++ b/solution.py
@@ -41,25 +41,34 @@
     return (p & 1) ^ (p >> 1), p >> 1
 
 
-def run(kernel, outs, *args, spaces=None, flops=0, moved=0, erfs=0, aliases=None, scratch=()):
-    vmem = pl.BlockSpec(memory_space=pltpu.VMEM)
-    specs = [vmem] * len(args)
-    for i, space in (spaces or {}).items():
-        specs[i] = pl.BlockSpec(memory_space=space)
-    single = not isinstance(outs, list)
-    shapes = [outs] if single else outs
-    moved = moved or sum(a.size * a.dtype.itemsize for a in args)
-    out = pl.pallas_call(
-        kernel,
-        out_shape=shapes,
-        in_specs=specs,
-        out_specs=[vmem] * len(shapes),
-        scratch_shapes=list(scratch),
-        input_output_aliases=aliases or {},
-        compiler_params=pltpu.CompilerParams(vmem_limit_bytes=LIMIT),
-        cost_estimate=pl.CostEstimate(flops=flops, bytes_accessed=moved, transcendentals=erfs),
-    )(*args)
-    return out[0] if single else out
+class Line:
+    def __init__(self):
+        self.last = None
+
+    def __call__(self, kernel, outs, *args, after=(), spaces=None, flops=0, moved=0, erfs=0, scratch=()):
+        waits = [*after] if self.last is None else [self.last, *after]
+        vmem = pl.BlockSpec(memory_space=pltpu.VMEM)
+        specs = [vmem] * len(args) + [pl.BlockSpec(memory_space=pl.ANY)] * len(waits)
+        for i, space in (spaces or {}).items():
+            specs[i] = pl.BlockSpec(memory_space=space)
+        single = not isinstance(outs, list)
+        shapes = [outs] if single else outs
+        moved = moved or sum(a.size * a.dtype.itemsize for a in args)
+
+        def body(*refs):
+            kernel(*refs[: len(args)], *refs[len(args) + len(waits) :])
+
+        out = pl.pallas_call(
+            body,
+            out_shape=shapes,
+            in_specs=specs,
+            out_specs=[vmem] * len(shapes),
+            scratch_shapes=list(scratch),
+            compiler_params=pltpu.CompilerParams(vmem_limit_bytes=LIMIT),
+            cost_estimate=pl.CostEstimate(flops=flops, bytes_accessed=moved, transcendentals=erfs),
+        )(*args, *waits)
+        self.last = out[0]
+        return out[0] if single else out
 
 
 def load_kernel(count, *refs):
@@ -78,19 +87,15 @@
         copy.wait()
 
 
-def load(weight, *extras, after=None):
+def load(run, weight, *extras):
     rows, columns = weight.shape
     count = len(extras)
     values = [pltpu.with_memory_space_constraint(v, pltpu.HBM) for v in (weight, *extras)]
-    spaces = {i: pltpu.HBM for i in range(1 + count)}
-    if after is not None:
-        values.append(after)
-        spaces[1 + count] = pl.ANY
     out = run(
         functools.partial(load_kernel, count),
         [pltpu.VMEM((4, rows, columns // 4), BF)] + [pltpu.VMEM(v.shape, v.dtype) for v in extras],
         *values,
-        spaces=spaces,
+        spaces={i: pltpu.HBM for i in range(1 + count)},
         moved=weight.size * 4,
         scratch=[pltpu.SemaphoreType.DMA((4 + count,))],
     )
@@ -104,9 +109,13 @@
         at += ref.shape[0]
 
 
-def pack(*values):
+def pack(run, *values):
     rows = sum(v.shape[0] for v in values)
     return run(pack_kernel, pltpu.VMEM((rows, values[0].shape[1]), BF), *values)
+
+
+def copied(run, value, *after):
+    return run(pack_kernel, pltpu.VMEM(value.shape, value.dtype), value, after=after)
 
 
 def side_bit(side):
@@ -124,7 +133,7 @@
     return pl.ds(pl.multiple_of((side_bit(q + 1) ^ near) * rows, rows), rows)
 
 
-def up_kernel(q, far, rows_ref, weight_ref, after, out_ref):
+def up_kernel(q, far, rows_ref, weight_ref, out_ref):
     half = out_ref.shape[0] // 2
     rows = jnp.concatenate([rows_ref[half_of(q, near, half)] for near in range(2)])
     quarter = quarter_of(q, far)
@@ -135,7 +144,7 @@
         out_ref[:, start:stop] = value.astype(out_ref.dtype)
 
 
-def second_kernel(kept_ref, got_ref, after, out_ref):
+def second_kernel(kept_ref, got_ref, out_ref):
     n = out_ref.shape[0]
     out_ref[...] = (kept_ref[n:] + got_ref[n:].astype(F32)).astype(BF)
 
@@ -159,10 +168,10 @@
     out_ref[...] = value.astype(BF)
 
 
-def add_down(q, far, rows_ref, weight_ref, from_ref, out_ref):
+def add_down(q, far, near_ref, far_ref, weight_ref, from_ref, out_ref):
     half = out_ref.shape[0] // 2
     value = lax.dot_general(
-        rows_ref[...],
+        jnp.concatenate([near_ref[...], far_ref[...]]),
         weight_ref[quarter_of(q, far)],
         (((1,), (1,)), ((), ())),
         preferred_element_type=F32,
@@ -173,16 +182,16 @@
         out_ref[at] = rows if from_ref is None else from_ref[at] + rows
 
 
-def down_own_kernel(q, one_ref, two_ref, weight_ref, out_ref):
-    add_down(q, 0, one_ref, weight_ref, None, out_ref)
-    add_down(q + 1, 0, two_ref, weight_ref, out_ref, out_ref)
-
-
-def down_kernel(q, total_ref, rows_ref, weight_ref, out_ref):
-    add_down(q, 1, rows_ref, weight_ref, total_ref, out_ref)
-
-
-def index_kernel(sizes_ref, map_ref, order_ref, after, out_ref, mid_ref):
+def down_own_kernel(q, one, one_more, two, two_more, weight_ref, out_ref):
+    add_down(q, 0, one, one_more, weight_ref, None, out_ref)
+    add_down(q + 1, 0, two, two_more, weight_ref, out_ref, out_ref)
+
+
+def down_kernel(q, total_ref, near_ref, far_ref, weight_ref, out_ref):
+    add_down(q, 1, near_ref, far_ref, weight_ref, total_ref, out_ref)
+
+
+def index_kernel(sizes_ref, map_ref, order_ref, out_ref, mid_ref):
     rows = order_ref.shape[1]
     reqs = sizes_ref.shape[1]
     own = rows // 8
@@ -252,90 +261,95 @@
     group = rows // 2
     chains = range(4)
 
+    run = Line()
     fetched = [from_chip(draft_rows, ahead) for ahead in (2, 1, 3)]
-    ups, draft = load(up_weight, draft_rows)
-    column = pack(draft, *fetched)
+    ups, draft = load(run, up_weight, draft_rows)
+    column = pack(run, draft, *fetched)
     beside = other_core(column)
 
     project_flops = 2 * group * width * part
 
-    def project(q, far, dtype, after):
+    def project(q, far, dtype):
         return run(
             functools.partial(up_kernel, q, far),
             pltpu.VMEM((group, part), dtype),
             column if q < 2 else beside,
             ups,
-            after,
-            spaces={2: pl.ANY},
             flops=project_flops,
         )
 
-    sent, after = [], column
-    for q in chains:
-        after = project(q, 1, BF, after)
-        sent.append(after)
-    got = [swap(sent[q], q) for q in chains]
-    kept = []
-    for q in chains:
-        after = project(q, 0, F32, after)
-        kept.append(after)
+    got = [swap(project(q, 1, BF), q) for q in chains]
+    kept = [project(q, 0, F32) for q in chains]
+    downs = load(run, down_weight.T)
     pick = run(
         index_kernel,
         pltpu.VMEM((rows, rows), BF),
         tree_sizes[None, :],
         draft_map[None, :],
         row_order[None, :],
-        after,
-        spaces={3: pl.ANY},
         flops=rows * rows * 64,
         scratch=[pltpu.VMEM((rows, rows), BF)],
     )
-    downs = load(down_weight.T, after=after)
 
     block = pltpu.VMEM((group // 2, part), BF)
     block32 = pltpu.VMEM((group // 2, part), F32)
-    came = [
-        swap(run(second_kernel, block, kept[q], got[q], after, spaces={2: pl.ANY}), (q + 1) % 4)
-        for q in chains
-    ]
+    came = [swap(run(second_kernel, block, kept[q], got[q]), (q + 1) % 4) for q in chains]
     third = [run(third_kernel, [block32, block], kept[q], got[q], came[q]) for q in chains]
     came = [swap(third[q][1], (q + 2) % 4) for q in chains]
     fourth = [run(fourth_kernel, [block32, block], third[q][0], came[q]) for q in chains]
     came = [swap(fourth[q][1], (q + 3) % 4) for q in chains]
     erfs = group // 2 * part
     hidden = [run(gelu_kernel, block, fourth[q][0], came[q], erfs=erfs) for q in chains]
-    came = [swap(hidden[q], (q + 1) % 4) for q in chains]
-    mine = [pack(hidden[q], came[q]) for q in chains]
-    came = [swap(mine[q], q) for q in chains]
+
     whole = pltpu.VMEM((group, width), F32)
-    sorted_rows = []
-    for i in range(2):
-        total = run(
-            functools.partial(down_own_kernel, 2 * i),
+
+    def down_own(q, *after):
+        return run(
+            functools.partial(down_own_kernel, q),
             whole,
-            mine[2 * i],
-            mine[2 * i + 1],
+            hidden[q],
+            more[q],
+            hidden[q + 1],
+            more[q + 1],
             downs,
+            after=after,
             flops=2 * project_flops,
         )
-        for q in (2 * i, 2 * i + 1):
-            total = run(
-                functools.partial(down_kernel, q),
-                whole,
-                    total,
-                came[q],
-                downs,
-                    flops=project_flops,
-            )
-        sorted_rows = run(
-            functools.partial(sort_kernel, i * group),
-            [whole, pltpu.VMEM((group, width), BF if i else F32)],
+
+    def down(q, total):
+        return run(
+            functools.partial(down_kernel, q),
+            whole,
+            total,
+            near[q],
+            far[q],
+            downs,
+            flops=project_flops,
+        )
+
+    def sort(at, total, dtype, *others):
+        return run(
+            functools.partial(sort_kernel, at),
+            [whole, pltpu.VMEM((group, width), dtype)],
             pick,
             total,
-            *sorted_rows,
+            *others,
             flops=3 * group * group * width,
         )
-    kept, out = sorted_rows
+
+    more = [swap(hidden[q], (q + 1) % 4) for q in chains]
+    near, far = {}, {}
+    for q, after in zip((1, 2, 3, 0), (hidden[3], more[0], more[1], more[2])):
+        near[q] = swap(copied(run, hidden[q], after), q)
+    far[1] = swap(copied(run, more[1], more[3]), 1)
+    one = down_own(0)
+    for q, after in zip((2, 3, 0), (near[1], near[2], near[3])):
+        far[q] = swap(copied(run, more[q], after), q)
+    two = down_own(2, near[0])
+    one = down(1, one)
+    two = down(3, down(2, two))
+    others = sort(group, two, F32)
+    kept, out = sort(0, down(0, one), BF, *others)
     row_block = pltpu.VMEM((own, width), BF)
     mine, one, two, three = run(
         deal_kernel,

time: 124 us -> 121 us (0.976)
  waiting for transfers between devices: 42.9 us -> 34.3 us
  starting transfers between devices: 48.4 us -> 54.4 us
    ppermute x24 -> x28, waiting for transfers between devices: 34.7 us -> 26.9 us  [swap(): return lax.ppermute(value, YZ, SWAPS[side])]
    ppermute x24 -> x28, starting transfers between devices: 36.1 us -> 41 us  [swap(): return lax.ppermute(value, YZ, SWAPS[side])]
    ppermute x2, starting transfers between devices: 3.46 us -> 4.91 us  [other_core(): return lax.ppermute(value, 'gr', [(i, i ^ 1) for i in range(8)])]
    pallas_call x42 -> x46, Pallas kernels: 32.2 us -> 32.2 us  [__call__(): pl.pallas_call(body, out_shape=shapes, in_specs=specs, out_specs=[vmem] *...]
  transfers between devices with their start and end apart: 32 -> 36, of which waited for: 14 -> 16; matrix products, arithmetic and copies ran while one was open for 0% -> 0% of each run, Pallas kernels for 24% -> 24%
where the time goes in v3:
time: 121 us
  starting transfers between devices  54.4 us (45%)
  waiting for transfers between devices  34.3 us (28%)
  Pallas kernels  32.2 us (27%)
    ppermute x28, starting transfers between devices, swap(): return lax.ppermute(value, YZ, SWAPS[side])  41 us
    pallas_call x46, Pallas kernels, __call__(): pl.pallas_call(body, out_shape=shapes, in_specs=specs, out_specs=[vmem] *...  32.2 us
    ppermute x28, waiting for transfers between devices, swap(): return lax.ppermute(value, YZ, SWAPS[side])  26.9 us
    ppermute x6, starting transfers between devices, from_chip(): return lax.ppermute(value, 'gr', pairs)  8.57 us
    ppermute x6, waiting for transfers between devices, from_chip(): return lax.ppermute(value, 'gr', pairs)  5.83 us
    ppermute x2, starting transfers between devices, other_core(): return lax.ppermute(value, 'gr', [(i, i ^ 1) for i in range(8)])  4.91 us
  transfers between devices with their start and end apart: 36, of which 16 were waited for; matrix products, arithmetic and copies ran while one was open for 0% of the time, Pallas kernels for 24%

profile of v3, /device:TPU:1, one launch (start us, length us, event | category | flops | bytes accessed | tf_op | source)
XLA Modules:
  0.0 121.3 jit_solution(17131577177460849994)
XLA Ops:
  0.0 3.6 %collective-permute-start = (bf16[64,928]{1,0:T(8,128)(2,1)}, bf16[64,928]{1,0:T(8,128)(2,1)S(1)}, u32[]{:S(2)}, u32[]{:S(2)}) collective-permute-start(bf16[64,928]{1,0:T(8,128)(2,1)} %refs_1_.1), channel_id=1, source_target_pairs={{64,0},{80,16},{96,32},{112,48},{0,64},{16,80},{32,96},{48,112},{6... | collective-permute-start | bytes 356360 | tf_op jit(solution)/shard_map/ppermute | solution.py:33
  5.0 4.7 %shard_map.64 = (bf16[4,928,1664]{2,1,0:T(8,128)(2,1)S(1)}, bf16[64,928]{1,0:T(8,128)(2,1)S(1)}) custom-call(bf16[928,6656]{1,0:T(8,128)(2,1)} %refs_0_.1, bf16[64,928]{1,0:T(8,128)(2,1)} %refs_1_.1), custom_call_target="tpu_custom_call" | custom-call | bytes 24707072 | tf_op jit(solution)/shard_map/pallas_call | solution.py:61
  9.8 2.3 %collective-permute-start.3 = (bf16[256,928]{1,0:T(8,128)(2,1)S(1)}, bf16[256,928]{1,0:T(8,128)(2,1)S(1)}, u32[]{:S(2)}, u32[]{:S(2)}) collective-permute-start(bf16[256,928]{1,0:T(8,128)(2,1)S(1)} %shard_map.65.refs_0_.refs_2_), channel_id=1, source_target_pairs={{0,16},{16,0},{32,48},{48,32},{64,80},{80,64},{96,112},{112,96},{1... | collective-permute-start | bytes 1425416 | tf_op jit(solution)/shard_map/ppermute | solution.py:37
  15.8 2.0 %collective-permute-start.8 = (bf16[256,1664]{1,0:T(8,128)(2,1)S(1)}, bf16[256,1664]{1,0:T(8,128)(2,1)S(1)}, u32[]{:S(2)}, u32[]{:S(2)}) collective-permute-start(bf16[256,1664]{1,0:T(8,128)(2,1)S(1)} %shard_map.67.refs_2_), channel_id=1, source_target_pairs={{0,12},{2,14},{1,13},{3,15},{4,8},{6,10},{5,9},{7,11},{8,4},{10,6}... | collective-permute-start | bytes 2555912 | tf_op jit(solution)/shard_map/ppermute | solution.py:28
  21.8 2.3 %collective-permute-start.6 = (bf16[256,1664]{1,0:T(8,128)(2,1)S(1)}, bf16[256,1664]{1,0:T(8,128)(2,1)S(1)}, u32[]{:S(2)}, u32[]{:S(2)}) collective-permute-start(bf16[256,1664]{1,0:T(8,128)(2,1)S(1)} %shard_map.69.refs_2_), channel_id=1, source_target_pairs={{0,3},{2,1},{1,2},{3,0},{4,7},{6,5},{5,6},{7,4},{8,11},{10,9},{9,1... | collective-permute-start | bytes 2555912 | tf_op jit(solution)/shard_map/ppermute | solution.py:28
  28.6 4.7 %shard_map.74.refs_3_.refs_4_ = bf16[4,928,1664]{2,1,0:T(8,128)(2,1)S(1)} custom-call(bf16[928,6656]{1,0:T(8,128)(2,1)} %bitcast.7, f32[256,1664]{1,0:T(8,128)S(1)} %shard_map.73.refs_1_.refs_0_), custom_call_target="tpu_custom_call" | custom-call | bytes 24707072 | tf_op jit(solution)/shard_map/pallas_call | solution.py:61
  34.0 2.8 %collective-permute-start.5 = (bf16[128,1664]{1,0:T(8,128)(2,1)S(1)}, bf16[128,1664]{1,0:T(8,128)(2,1)S(1)}, u32[]{:S(2)}, u32[]{:S(2)}) collective-permute-start(bf16[128,1664]{1,0:T(8,128)(2,1)S(1)} %shard_map.76.refs_2_), channel_id=1, source_target_pairs={{0,12},{2,14},{1,13},{3,15},{4,8},{6,10},{5,9},{7,11},{8,4},{10,6}... | collective-permute-start | bytes 1277960 | tf_op jit(solution)/shard_map/ppermute | solution.py:28
  39.3 3.5 %collective-permute-start.11 = (bf16[128,1664]{1,0:T(8,128)(2,1)S(1)}, bf16[128,1664]{1,0:T(8,128)(2,1)S(1)}, u32[]{:S(2)}, u32[]{:S(2)}) collective-permute-start(bf16[128,1664]{1,0:T(8,128)(2,1)S(1)} %shard_map.78.refs_2_), channel_id=1, source_target_pairs={{0,3},{2,1},{1,2},{3,0},{4,7},{6,5},{5,6},{7,4},{8,11},{10,9},{9,1... | collective-permute-start | bytes 1277960 | tf_op jit(solution)/shard_map/ppermute | solution.py:28
  43.4 2.3 %collective-permute-done.5.refs_2_ = bf16[128,1664]{1,0:T(8,128)(2,1)S(1)} collective-permute-done((bf16[128,1664]{1,0:T(8,128)(2,1)S(1)}, bf16[128,1664]{1,0:T(8,128)(2,1)S(1)}, u32[]{:S(2)}, u32[]{:S(2)}) %collective-permute-start.5) | collective-permute-done | bytes 426016 | tf_op jit(solution)/shard_map/ppermute | solution.py:28
  45.9 2.0 %collective-permute-start.9 = (bf16[128,1664]{1,0:T(8,128)(2,1)S(1)}, bf16[128,1664]{1,0:T(8,128)(2,1)S(1)}, u32[]{:S(2)}, u32[]{:S(2)}) collective-permute-start(bf16[128,1664]{1,0:T(8,128)(2,1)S(1)} %get-tuple-element.34), channel_id=1, source_target_pairs={{0,2},{2,0},{1,3},{3,1},{4,6},{6,4},{5,7},{7,5},{8,10},{10,8},{9,1... | collective-permute-start | bytes 1277960 | tf_op jit(solution)/shard_map/ppermute | solution.py:28
  48.1 3.5 %collective-permute-start.16 = (bf16[128,1664]{1,0:T(8,128)(2,1)S(1)}, bf16[128,1664]{1,0:T(8,128)(2,1)S(1)}, u32[]{:S(2)}, u32[]{:S(2)}) collective-permute-start(bf16[128,1664]{1,0:T(8,128)(2,1)S(1)} %get-tuple-element.42), channel_id=1, source_target_pairs={{0,3},{2,1},{1,2},{3,0},{4,7},{6,5},{5,6},{7,4},{8,11},{10,9},{9,1... | collective-permute-start | bytes 1277960 | tf_op jit(solution)/shard_map/ppermute | solution.py:28
  54.2 2.8 %collective-permute-done.9.refs_1_ = bf16[128,1664]{1,0:T(8,128)(2,1)S(1)} collective-permute-done((bf16[128,1664]{1,0:T(8,128)(2,1)S(1)}, bf16[128,1664]{1,0:T(8,128)(2,1)S(1)}, u32[]{:S(2)}, u32[]{:S(2)}) %collective-permute-start.9) | collective-permute-done | bytes 426016 | tf_op jit(solution)/shard_map/ppermute | solution.py:28
  57.1 3.5 %collective-permute-start.13 = (bf16[128,1664]{1,0:T(8,128)(2,1)S(1)}, bf16[128,1664]{1,0:T(8,128)(2,1)S(1)}, u32[]{:S(2)}, u32[]{:S(2)}) collective-permute-start(bf16[128,1664]{1,0:T(8,128)(2,1)S(1)} %get-tuple-element.39), channel_id=1, source_target_pairs={{0,3},{2,1},{1,2},{3,0},{4,7},{6,5},{5,6},{7,4},{8,11},{10,9},{9,1... | collective-permute-start | bytes 1277960 | tf_op jit(solution)/shard_map/ppermute | solution.py:28
  63.5 5.9 %collective-permute-done.13.refs_1_ = bf16[128,1664]{1,0:T(8,128)(2,1)S(1)} collective-permute-done((bf16[128,1664]{1,0:T(8,128)(2,1)S(1)}, bf16[128,1664]{1,0:T(8,128)(2,1)S(1)}, u32[]{:S(2)}, u32[]{:S(2)}) %collective-permute-start.13) | collective-permute-done | bytes 426016 | tf_op jit(solution)/shard_map/ppermute | solution.py:28
  74.3 2.0 %collective-permute-start.24 = (bf16[128,1664]{1,0:T(8,128)(2,1)S(1)}, bf16[128,1664]{1,0:T(8,128)(2,1)S(1)}, u32[]{:S(2)}, u32[]{:S(2)}) collective-permute-start(bf16[128,1664]{1,0:T(8,128)(2,1)S(1)} %shard_map.92.refs_1_), channel_id=1, source_target_pairs={{0,12},{2,14},{1,13},{3,15},{4,8},{6,10},{5,9},{7,11},{8,4},{10,6}... | collective-permute-start | bytes 1277960 | tf_op jit(solution)/shard_map/ppermute | solution.py:28
  76.3 6.6 %collective-permute-done.17.refs_2_.refs_1_.refs_0_ = bf16[128,1664]{1,0:T(8,128)(2,1)S(1)} collective-permute-done((bf16[128,1664]{1,0:T(8,128)(2,1)S(1)}, bf16[128,1664]{1,0:T(8,128)(2,1)S(1)}, u32[]{:S(2)}, u32[]{:S(2)}) %collective-permute-start.17) | collective-permute-done | bytes 426016 | tf_op jit(solution)/shard_map/ppermute | solution.py:28
  86.2 2.1 %shard_map.97.refs_1_.refs_0_ = f32[256,928]{1,0:T(8,128)S(1)} custom-call(bf16[128,1664]{1,0:T(8,128)(2,1)S(1)} %shard_map.88.refs_2_.refs_0_, bf16[128,1664]{1,0:T(8,128)(2,1)S(1)} %collective-permute-done.17.refs_2_.refs_1_.refs_0_, bf16[128,1664]{1,0:T(8,128)(2,1)S(1)} %shard_map.89.refs_2_.refs_0_, ...), custom_call_target="tpu_custom_call" | custom-call | flops 1581252608 | bytes 14057472 | tf_op jit(solution)/shard_map/pallas_call | solution.py:61
  88.3 3.8 %collective-permute-done.24.refs_2_.refs_1_ = bf16[128,1664]{1,0:T(8,128)(2,1)S(1)} collective-permute-done((bf16[128,1664]{1,0:T(8,128)(2,1)S(1)}, bf16[128,1664]{1,0:T(8,128)(2,1)S(1)}, u32[]{:S(2)}, u32[]{:S(2)}) %collective-permute-start.24) | collective-permute-done | bytes 426016 | tf_op jit(solution)/shard_map/ppermute | solution.py:28
  94.8 2.1 %shard_map.101.refs_4_.refs_0_ = f32[256,928]{1,0:T(8,128)S(1)} custom-call(bf16[128,1664]{1,0:T(8,128)(2,1)S(1)} %shard_map.90.refs_2_.refs_0_, bf16[128,1664]{1,0:T(8,128)(2,1)S(1)} %collective-permute-done.22.refs_2_.refs_0_.refs_1_, bf16[128,1664]{1,0:T(8,128)(2,1)S(1)} %shard_map.91.refs_1_.refs_2_.refs_0_, ...), custom_call_target="tpu_custom_call" | custom-call | flops 1581252608 | bytes 14057472 | tf_op jit(solution)/shard_map/pallas_call | solution.py:61
  96.9 4.3 %collective-permute-done.25.refs_2_ = bf16[128,1664]{1,0:T(8,128)(2,1)S(1)} collective-permute-done((bf16[128,1664]{1,0:T(8,128)(2,1)S(1)}, bf16[128,1664]{1,0:T(8,128)(2,1)S(1)}, u32[]{:S(2)}, u32[]{:S(2)}) %collective-permute-start.25) | collective-permute-done | bytes 426016 | tf_op jit(solution)/shard_map/ppermute | solution.py:28
  107.1 2.6 %collective-permute-start.32 = (bf16[256,928]{1,0:T(8,128)(2,1)S(1)}, bf16[256,928]{1,0:T(8,128)(2,1)S(1)}, u32[]{:S(2)}, u32[]{:S(2)}) collective-permute-start(bf16[256,928]{1,0:T(8,128)(2,1)S(1)} %get-tuple-element.52), channel_id=1, source_target_pairs={{0,16},{16,0},{32,48},{48,32},{64,80},{80,64},{96,112},{112,96},{1... | collective-permute-start | bytes 1425416 | tf_op jit(solution)/shard_map/ppermute | solution.py:37
  111.3 2.1 %collective-permute-start.33 = (bf16[64,928]{1,0:T(8,128)(2,1)S(1)}, bf16[64,928]{1,0:T(8,128)(2,1)S(1)}, u32[]{:S(2)}, u32[]{:S(2)}) collective-permute-start(bf16[64,928]{1,0:T(8,128)(2,1)S(1)} %get-tuple-element.54), channel_id=1, source_target_pairs={{64,0},{80,16},{96,32},{112,48},{0,64},{16,80},{32,96},{48,112},{6... | collective-permute-start | bytes 356360 | tf_op jit(solution)/shard_map/ppermute | solution.py:33
  114.8 2.8 %collective-permute-done.33.refs_1_ = bf16[64,928]{1,0:T(8,128)(2,1)S(1)} collective-permute-done((bf16[64,928]{1,0:T(8,128)(2,1)S(1)}, bf16[64,928]{1,0:T(8,128)(2,1)S(1)}, u32[]{:S(2)}, u32[]{:S(2)}) %collective-permute-start.33) | collective-permute-done | bytes 118816 | tf_op jit(solution)/shard_map/ppermute | solution.py:33
  117.6 2.1 %collective-permute-done.34.refs_2_ = bf16[64,928]{1,0:T(8,128)(2,1)S(1)} collective-permute-done((bf16[64,928]{1,0:T(8,128)(2,1)S(1)}, bf16[64,928]{1,0:T(8,128)(2,1)S(1)}, u32[]{:S(2)}, u32[]{:S(2)}) %collective-permute-start.34) | collective-permute-done | bytes 118816 | tf_op jit(solution)/shard_map/ppermute | solution.py:33
  (100 shorter events, 44.9 us)
Async XLA Ops:
  13.3 20.6 %collective-permute-start.4 = (bf16[256,1664]{1,0:T(8,128)(2,1)S(1)}, bf16[256,1664]{1,0:T(8,128)(2,1)S(1)}, u32[]{:S(2)}, u32[]{:S(2)}) collective-permute-start(bf16[256,1664]{1,0:T(8,128)(2,1)S(1)} %shard_map.66.refs_2_), channel_id=1, source_target_pairs={{0,4},{2,6},{1,5},{3,7},{4,0},{6,2},{5,1},{7,3},{8,12},{10,14},{9,... | collective-permute-start | bytes 2555912 | tf_op jit(solution)/shard_map/ppermute | solution.py:28
  15.8 21.5 %collective-permute-start.8 = (bf16[256,1664]{1,0:T(8,128)(2,1)S(1)}, bf16[256,1664]{1,0:T(8,128)(2,1)S(1)}, u32[]{:S(2)}, u32[]{:S(2)}) collective-permute-start(bf16[256,1664]{1,0:T(8,128)(2,1)S(1)} %shard_map.67.refs_2_), channel_id=1, source_target_pairs={{0,12},{2,14},{1,13},{3,15},{4,8},{6,10},{5,9},{7,11},{8,4},{10,6}... | collective-permute-start | bytes 2555912 | tf_op jit(solution)/shard_map/ppermute | solution.py:28
  18.9 20.4 %collective-permute-start.7 = (bf16[256,1664]{1,0:T(8,128)(2,1)S(1)}, bf16[256,1664]{1,0:T(8,128)(2,1)S(1)}, u32[]{:S(2)}, u32[]{:S(2)}) collective-permute-start(bf16[256,1664]{1,0:T(8,128)(2,1)S(1)} %shard_map.68.refs_2_), channel_id=1, source_target_pairs={{0,2},{2,0},{1,3},{3,1},{4,6},{6,4},{5,7},{7,5},{8,10},{10,8},{9,1... | collective-permute-start | bytes 2555912 | tf_op jit(solution)/shard_map/ppermute | solution.py:28
  21.8 21.1 %collective-permute-start.6 = (bf16[256,1664]{1,0:T(8,128)(2,1)S(1)}, bf16[256,1664]{1,0:T(8,128)(2,1)S(1)}, u32[]{:S(2)}, u32[]{:S(2)}) collective-permute-start(bf16[256,1664]{1,0:T(8,128)(2,1)S(1)} %shard_map.69.refs_2_), channel_id=1, source_target_pairs={{0,3},{2,1},{1,2},{3,0},{4,7},{6,5},{5,6},{7,4},{8,11},{10,9},{9,1... | collective-permute-start | bytes 2555912 | tf_op jit(solution)/shard_map/ppermute | solution.py:28
  34.0 11.7 %collective-permute-start.5 = (bf16[128,1664]{1,0:T(8,128)(2,1)S(1)}, bf16[128,1664]{1,0:T(8,128)(2,1)S(1)}, u32[]{:S(2)}, u32[]{:S(2)}) collective-permute-start(bf16[128,1664]{1,0:T(8,128)(2,1)S(1)} %shard_map.76.refs_2_), channel_id=1, source_target_pairs={{0,12},{2,14},{1,13},{3,15},{4,8},{6,10},{5,9},{7,11},{8,4},{10,6}... | collective-permute-start | bytes 1277960 | tf_op jit(solution)/shard_map/ppermute | solution.py:28
  37.4 10.5 %collective-permute-start.12 = (bf16[128,1664]{1,0:T(8,128)(2,1)S(1)}, bf16[128,1664]{1,0:T(8,128)(2,1)S(1)}, u32[]{:S(2)}, u32[]{:S(2)}) collective-permute-start(bf16[128,1664]{1,0:T(8,128)(2,1)S(1)} %shard_map.77.refs_2_), channel_id=1, source_target_pairs={{0,2},{2,0},{1,3},{3,1},{4,6},{6,4},{5,7},{7,5},{8,10},{10,8},{9,1... | collective-permute-start | bytes 1277960 | tf_op jit(solution)/shard_map/ppermute | solution.py:28
  39.3 12.3 %collective-permute-start.11 = (bf16[128,1664]{1,0:T(8,128)(2,1)S(1)}, bf16[128,1664]{1,0:T(8,128)(2,1)S(1)}, u32[]{:S(2)}, u32[]{:S(2)}) collective-permute-start(bf16[128,1664]{1,0:T(8,128)(2,1)S(1)} %shard_map.78.refs_2_), channel_id=1, source_target_pairs={{0,3},{2,1},{1,2},{3,0},{4,7},{6,5},{5,6},{7,4},{8,11},{10,9},{9,1... | collective-permute-start | bytes 1277960 | tf_op jit(solution)/shard_map/ppermute | solution.py:28
  45.9 11.2 %collective-permute-start.9 = (bf16[128,1664]{1,0:T(8,128)(2,1)S(1)}, bf16[128,1664]{1,0:T(8,128)(2,1)S(1)}, u32[]{:S(2)}, u32[]{:S(2)}) collective-permute-start(bf16[128,1664]{1,0:T(8,128)(2,1)S(1)} %get-tuple-element.34), channel_id=1, source_target_pairs={{0,2},{2,0},{1,3},{3,1},{4,6},{6,4},{5,7},{7,5},{8,10},{10,8},{9,1... | collective-permute-start | bytes 1277960 | tf_op jit(solution)/shard_map/ppermute | solution.py:28
  48.1 12.5 %collective-permute-start.16 = (bf16[128,1664]{1,0:T(8,128)(2,1)S(1)}, bf16[128,1664]{1,0:T(8,128)(2,1)S(1)}, u32[]{:S(2)}, u32[]{:S(2)}) collective-permute-start(bf16[128,1664]{1,0:T(8,128)(2,1)S(1)} %get-tuple-element.42), channel_id=1, source_target_pairs={{0,3},{2,1},{1,2},{3,0},{4,7},{6,5},{5,6},{7,4},{8,11},{10,9},{9,1... | collective-permute-start | bytes 1277960 | tf_op jit(solution)/shard_map/ppermute | solution.py:28
  53.0 10.2 %collective-permute-start.14 = (bf16[128,1664]{1,0:T(8,128)(2,1)S(1)}, bf16[128,1664]{1,0:T(8,128)(2,1)S(1)}, u32[]{:S(2)}, u32[]{:S(2)}) collective-permute-start(bf16[128,1664]{1,0:T(8,128)(2,1)S(1)} %get-tuple-element.40), channel_id=1, source_target_pairs={{0,12},{2,14},{1,13},{3,15},{4,8},{6,10},{5,9},{7,11},{8,4},{10,6}... | collective-permute-start | bytes 1277960 | tf_op jit(solution)/shard_map/ppermute | solution.py:28
  57.1 12.3 %collective-permute-start.13 = (bf16[128,1664]{1,0:T(8,128)(2,1)S(1)}, bf16[128,1664]{1,0:T(8,128)(2,1)S(1)}, u32[]{:S(2)}, u32[]{:S(2)}) collective-permute-start(bf16[128,1664]{1,0:T(8,128)(2,1)S(1)} %get-tuple-element.39), channel_id=1, source_target_pairs={{0,3},{2,1},{1,2},{3,0},{4,7},{6,5},{5,6},{7,4},{8,11},{10,9},{9,1... | collective-permute-start | bytes 1277960 | tf_op jit(solution)/shard_map/ppermute | solution.py:28
  60.7 10.0 %collective-permute-start.18 = (bf16[128,1664]{1,0:T(8,128)(2,1)S(1)}, bf16[128,1664]{1,0:T(8,128)(2,1)S(1)}, u32[]{:S(2)}, u32[]{:S(2)}) collective-permute-start(bf16[128,1664]{1,0:T(8,128)(2,1)S(1)} %get-tuple-element.46), channel_id=1, source_target_pairs={{0,4},{2,6},{1,5},{3,7},{4,0},{6,2},{5,1},{7,3},{8,12},{10,14},{9,... | collective-permute-start | bytes 1277960 | tf_op jit(solution)/shard_map/ppermute | solution.py:28
  61.3 10.7 %collective-permute-start.21 = (bf16[128,1664]{1,0:T(8,128)(2,1)S(1)}, bf16[128,1664]{1,0:T(8,128)(2,1)S(1)}, u32[]{:S(2)}, u32[]{:S(2)}) collective-permute-start(bf16[128,1664]{1,0:T(8,128)(2,1)S(1)} %get-tuple-element.48), channel_id=1, source_target_pairs={{0,12},{2,14},{1,13},{3,15},{4,8},{6,10},{5,9},{7,11},{8,4},{10,6}... | collective-permute-start | bytes 1277960 | tf_op jit(solution)/shard_map/ppermute | solution.py:28
  63.3 10.6 %collective-permute-start.20 = (bf16[128,1664]{1,0:T(8,128)(2,1)S(1)}, bf16[128,1664]{1,0:T(8,128)(2,1)S(1)}, u32[]{:S(2)}, u32[]{:S(2)}) collective-permute-start(bf16[128,1664]{1,0:T(8,128)(2,1)S(1)} %get-tuple-element.47), channel_id=1, source_target_pairs={{0,2},{2,0},{1,3},{3,1},{4,6},{6,4},{5,7},{7,5},{8,10},{10,8},{9,1... | collective-permute-start | bytes 1277960 | tf_op jit(solution)/shard_map/ppermute | solution.py:28
  69.7 13.2 %collective-permute-start.17 = (bf16[128,1664]{1,0:T(8,128)(2,1)S(1)}, bf16[128,1664]{1,0:T(8,128)(2,1)S(1)}, u32[]{:S(2)}, u32[]{:S(2)}) collective-permute-start(bf16[128,1664]{1,0:T(8,128)(2,1)S(1)} %shard_map.88.refs_2_.refs_0_), channel_id=1, source_target_pairs={{0,12},{2,14},{1,13},{3,15},{4,8},{6,10},{5,9},{7,11},{8,4},{10,6}... | collective-permute-start | bytes 1277960 | tf_op jit(solution)/shard_map/ppermute | solution.py:28
  71.0 12.3 %collective-permute-start.19 = (bf16[128,1664]{1,0:T(8,128)(2,1)S(1)}, bf16[128,1664]{1,0:T(8,128)(2,1)S(1)}, u32[]{:S(2)}, u32[]{:S(2)}) collective-permute-start(bf16[128,1664]{1,0:T(8,128)(2,1)S(1)} %shard_map.89.refs_2_.refs_0_), channel_id=1, source_target_pairs={{0,2},{2,0},{1,3},{3,1},{4,6},{6,4},{5,7},{7,5},{8,10},{10,8},{9,1... | collective-permute-start | bytes 1277960 | tf_op jit(solution)/shard_map/ppermute | solution.py:28
  72.2 13.0 %collective-permute-start.22 = (bf16[128,1664]{1,0:T(8,128)(2,1)S(1)}, bf16[128,1664]{1,0:T(8,128)(2,1)S(1)}, u32[]{:S(2)}, u32[]{:S(2)}) collective-permute-start(bf16[128,1664]{1,0:T(8,128)(2,1)S(1)} %shard_map.90.refs_2_.refs_0_), channel_id=1, source_target_pairs={{0,3},{2,1},{1,2},{3,0},{4,7},{6,5},{5,6},{7,4},{8,11},{10,9},{9,1... | collective-permute-start | bytes 1277960 | tf_op jit(solution)/shard_map/ppermute | solution.py:28
  74.1 11.3 %collective-permute-start.23 = (bf16[128,1664]{1,0:T(8,128)(2,1)S(1)}, bf16[128,1664]{1,0:T(8,128)(2,1)S(1)}, u32[]{:S(2)}, u32[]{:S(2)}) collective-permute-start(bf16[128,1664]{1,0:T(8,128)(2,1)S(1)} %shard_map.91.refs_1_.refs_2_.refs_0_), channel_id=1, source_target_pairs={{0,4},{2,6},{1,5},{3,7},{4,0},{6,2},{5,1},{7,3},{8,12},{10,14},{9,... | collective-permute-start | bytes 1277960 | tf_op jit(solution)/shard_map/ppermute | solution.py:28
  74.3 17.8 %collective-permute-start.24 = (bf16[128,1664]{1,0:T(8,128)(2,1)S(1)}, bf16[128,1664]{1,0:T(8,128)(2,1)S(1)}, u32[]{:S(2)}, u32[]{:S(2)}) collective-permute-start(bf16[128,1664]{1,0:T(8,128)(2,1)S(1)} %shard_map.92.refs_1_), channel_id=1, source_target_pairs={{0,12},{2,14},{1,13},{3,15},{4,8},{6,10},{5,9},{7,11},{8,4},{10,6}... | collective-permute-start | bytes 1277960 | tf_op jit(solution)/shard_map/ppermute | solution.py:28
  83.4 10.9 %collective-permute-start.27 = (bf16[128,1664]{1,0:T(8,128)(2,1)S(1)}, bf16[128,1664]{1,0:T(8,128)(2,1)S(1)}, u32[]{:S(2)}, u32[]{:S(2)}) collective-permute-start(bf16[128,1664]{1,0:T(8,128)(2,1)S(1)} %shard_map.94.refs_1_), channel_id=1, source_target_pairs={{0,3},{2,1},{1,2},{3,0},{4,7},{6,5},{5,6},{7,4},{8,11},{10,9},{9,1... | collective-permute-start | bytes 1277960 | tf_op jit(solution)/shard_map/ppermute | solution.py:28
  85.5 15.7 %collective-permute-start.25 = (bf16[128,1664]{1,0:T(8,128)(2,1)S(1)}, bf16[128,1664]{1,0:T(8,128)(2,1)S(1)}, u32[]{:S(2)}, u32[]{:S(2)}) collective-permute-start(bf16[128,1664]{1,0:T(8,128)(2,1)S(1)} %shard_map.96.refs_5_), channel_id=1, source_target_pairs={{0,12},{2,14},{1,13},{3,15},{4,8},{6,10},{5,9},{7,11},{8,4},{10,6}... | collective-permute-start | bytes 1277960 | tf_op jit(solution)/shard_map/ppermute | solution.py:28
  92.1 10.3 %collective-permute-start.30 = (bf16[128,1664]{1,0:T(8,128)(2,1)S(1)}, bf16[128,1664]{1,0:T(8,128)(2,1)S(1)}, u32[]{:S(2)}, u32[]{:S(2)}) collective-permute-start(bf16[128,1664]{1,0:T(8,128)(2,1)S(1)} %shard_map.98.refs_1_), channel_id=1, source_target_pairs={{0,2},{2,0},{1,3},{3,1},{4,6},{6,4},{5,7},{7,5},{8,10},{10,8},{9,1... | collective-permute-start | bytes 1277960 | tf_op jit(solution)/shard_map/ppermute | solution.py:28
  92.5 11.0 %collective-permute-start.31 = (bf16[128,1664]{1,0:T(8,128)(2,1)S(1)}, bf16[128,1664]{1,0:T(8,128)(2,1)S(1)}, u32[]{:S(2)}, u32[]{:S(2)}) collective-permute-start(bf16[128,1664]{1,0:T(8,128)(2,1)S(1)} %shard_map.99.refs_1_), channel_id=1, source_target_pairs={{0,3},{2,1},{1,2},{3,0},{4,7},{6,5},{5,6},{7,4},{8,11},{10,9},{9,1... | collective-permute-start | bytes 1277960 | tf_op jit(solution)/shard_map/ppermute | solution.py:28
  94.4 10.9 %collective-permute-start.29 = (bf16[128,1664]{1,0:T(8,128)(2,1)S(1)}, bf16[128,1664]{1,0:T(8,128)(2,1)S(1)}, u32[]{:S(2)}, u32[]{:S(2)}) collective-permute-start(bf16[128,1664]{1,0:T(8,128)(2,1)S(1)} %shard_map.100.refs_5_), channel_id=1, source_target_pairs={{0,4},{2,6},{1,5},{3,7},{4,0},{6,2},{5,1},{7,3},{8,12},{10,14},{9,... | collective-permute-start | bytes 1277960 | tf_op jit(solution)/shard_map/ppermute | solution.py:28
  (15 other events, 104.9 us)

commit v4 on v3

--- a/solution.py
+++ b/solution.py
@@ -222,20 +222,18 @@
         out_ref[t * own : (t + 1) * own] = mid_ref[pl.ds(pl.multiple_of(block * own, own), own)]
 
 
-def sort_kernel(at, pick_ref, value_ref, *refs):
-    kept_ref, out_ref = refs[-2:]
-    half = kept_ref.shape[0]
+def sort_kernel(at, side, exact, pick_ref, value_ref, *refs):
+    out_ref = refs[-1]
+    half = out_ref.shape[0]
     value = value_ref[...]
     high = value.astype(BF)
-    low = (value - high.astype(F32)).astype(BF)
-    pick = pick_ref[:, at : at + value.shape[0]]
-    kept = jnp.dot(pick[:half], high, preferred_element_type=F32)
-    kept += jnp.dot(pick[:half], low, preferred_element_type=F32)
-    out = jnp.dot(pick[half:], high, preferred_element_type=F32)
-    if len(refs) == 4:
-        kept += refs[0][...]
-        out += refs[1][...]
-    kept_ref[...] = kept
+    pick = pick_ref[side * half : (side + 1) * half, at : at + value.shape[0]]
+    out = jnp.dot(pick, high, preferred_element_type=F32)
+    if exact:
+        low = (value - high.astype(F32)).astype(BF)
+        out += jnp.dot(pick, low, preferred_element_type=F32)
+    for ref in refs[:-1]:
+        out += ref[...]
     out_ref[...] = out.astype(out_ref.dtype)
 
 
@@ -327,14 +325,14 @@
             flops=project_flops,
         )
 
-    def sort(at, total, dtype, *others):
+    def sort(at, side, total, dtype, *others):
         return run(
-            functools.partial(sort_kernel, at),
-            [whole, pltpu.VMEM((group, width), dtype)],
+            functools.partial(sort_kernel, at, side, side == 0),
+            pltpu.VMEM((group, width), dtype),
             pick,
             total,
             *others,
-            flops=3 * group * group * width,
+            flops=2 * group * group * width,
         )
 
     more = [swap(hidden[q], (q + 1) % 4) for q in chains]
@@ -348,14 +346,16 @@
     two = down_own(2, near[0])
     one = down(1, one)
     two = down(3, down(2, two))
-    others = sort(group, two, F32)
-    kept, out = sort(0, down(0, one), BF, *others)
+    other = sort(group, 1, two, F32)
+    one = down(0, one)
+    out = other_core(sort(0, 1, one, BF, other))
+    kept = sort(0, 0, one, F32, sort(group, 0, two, F32))
     row_block = pltpu.VMEM((own, width), BF)
     mine, one, two, three = run(
         deal_kernel,
         [pltpu.VMEM((own, width), F32), row_block, row_block, row_block],
         kept,
-        other_core(out),
+        out,
     )
     arrived = [from_chip(value, ahead) for ahead, value in ((2, two), (1, three), (3, one))]
     return run(last_kernel, jax.ShapeDtypeStruct((own, width), BF), mine, *arrived)

time: 121 us -> 121 us (level)
    pallas_call x46 -> x48, Pallas kernels: 32.2 us -> 32.5 us  [__call__(): pl.pallas_call(body, out_shape=shapes, in_specs=specs, out_specs=[vmem] *...]
  transfers between devices with their start and end apart: 36 -> 36, of which waited for: 16 -> 16; matrix products, arithmetic and copies ran while one was open for 0% -> 0% of each run, Pallas kernels for 24% -> 25%
where the time goes in v4:
time: 121 us
  starting transfers between devices  54.4 us (45%)
  waiting for transfers between devices  33.4 us (28%)
  Pallas kernels  32.5 us (27%)
    ppermute x28, starting transfers between devices, swap(): return lax.ppermute(value, YZ, SWAPS[side])  41 us
    pallas_call x48, Pallas kernels, __call__(): pl.pallas_call(body, out_shape=shapes, in_specs=specs, out_specs=[vmem] *...  32.5 us
    ppermute x28, waiting for transfers between devices, swap(): return lax.ppermute(value, YZ, SWAPS[side])  26.9 us
    ppermute x6, starting transfers between devices, from_chip(): return lax.ppermute(value, 'gr', pairs)  8.58 us
    ppermute x6, waiting for transfers between devices, from_chip(): return lax.ppermute(value, 'gr', pairs)  5.82 us
    ppermute x2, starting transfers between devices, other_core(): return lax.ppermute(value, 'gr', [(i, i ^ 1) for i in range(8)])  4.91 us
  transfers between devices with their start and end apart: 36, of which 16 were waited for; matrix products, arithmetic and copies ran while one was open for 0% of the time, Pallas kernels for 25%

profile of v4, /device:TPU:1, one launch (start us, length us, event | category | flops | bytes accessed | tf_op | source)
XLA Modules:
  0.0 120.7 jit_solution(8191933147111457270)
XLA Ops:
  0.0 3.6 %collective-permute-start = (bf16[64,928]{1,0:T(8,128)(2,1)}, bf16[64,928]{1,0:T(8,128)(2,1)S(1)}, u32[]{:S(2)}, u32[]{:S(2)}) collective-permute-start(bf16[64,928]{1,0:T(8,128)(2,1)} %refs_1_.1), channel_id=1, source_target_pairs={{64,0},{80,16},{96,32},{112,48},{0,64},{16,80},{32,96},{48,112},{6... | collective-permute-start | bytes 356360 | tf_op jit(solution)/shard_map/ppermute | solution.py:33
  5.0 4.7 %shard_map.64 = (bf16[4,928,1664]{2,1,0:T(8,128)(2,1)S(1)}, bf16[64,928]{1,0:T(8,128)(2,1)S(1)}) custom-call(bf16[928,6656]{1,0:T(8,128)(2,1)} %refs_0_.1, bf16[64,928]{1,0:T(8,128)(2,1)} %refs_1_.1), custom_call_target="tpu_custom_call" | custom-call | bytes 24707072 | tf_op jit(solution)/shard_map/pallas_call | solution.py:61
  9.8 2.3 %collective-permute-start.3 = (bf16[256,928]{1,0:T(8,128)(2,1)S(1)}, bf16[256,928]{1,0:T(8,128)(2,1)S(1)}, u32[]{:S(2)}, u32[]{:S(2)}) collective-permute-start(bf16[256,928]{1,0:T(8,128)(2,1)S(1)} %shard_map.65.refs_0_.refs_2_), channel_id=1, source_target_pairs={{0,16},{16,0},{32,48},{48,32},{64,80},{80,64},{96,112},{112,96},{1... | collective-permute-start | bytes 1425416 | tf_op jit(solution)/shard_map/ppermute | solution.py:37
  15.8 2.0 %collective-permute-start.8 = (bf16[256,1664]{1,0:T(8,128)(2,1)S(1)}, bf16[256,1664]{1,0:T(8,128)(2,1)S(1)}, u32[]{:S(2)}, u32[]{:S(2)}) collective-permute-start(bf16[256,1664]{1,0:T(8,128)(2,1)S(1)} %shard_map.67.refs_2_), channel_id=1, source_target_pairs={{0,12},{2,14},{1,13},{3,15},{4,8},{6,10},{5,9},{7,11},{8,4},{10,6}... | collective-permute-start | bytes 2555912 | tf_op jit(solution)/shard_map/ppermute | solution.py:28
  21.8 2.3 %collective-permute-start.6 = (bf16[256,1664]{1,0:T(8,128)(2,1)S(1)}, bf16[256,1664]{1,0:T(8,128)(2,1)S(1)}, u32[]{:S(2)}, u32[]{:S(2)}) collective-permute-start(bf16[256,1664]{1,0:T(8,128)(2,1)S(1)} %shard_map.69.refs_2_), channel_id=1, source_target_pairs={{0,3},{2,1},{1,2},{3,0},{4,7},{6,5},{5,6},{7,4},{8,11},{10,9},{9,1... | collective-permute-start | bytes 2555912 | tf_op jit(solution)/shard_map/ppermute | solution.py:28
  28.6 4.7 %shard_map.74.refs_3_.refs_4_ = bf16[4,928,1664]{2,1,0:T(8,128)(2,1)S(1)} custom-call(bf16[928,6656]{1,0:T(8,128)(2,1)} %bitcast.7, f32[256,1664]{1,0:T(8,128)S(1)} %shard_map.73.refs_1_.refs_0_), custom_call_target="tpu_custom_call" | custom-call | bytes 24707072 | tf_op jit(solution)/shard_map/pallas_call | solution.py:61
  34.0 2.8 %collective-permute-start.5 = (bf16[128,1664]{1,0:T(8,128)(2,1)S(1)}, bf16[128,1664]{1,0:T(8,128)(2,1)S(1)}, u32[]{:S(2)}, u32[]{:S(2)}) collective-permute-start(bf16[128,1664]{1,0:T(8,128)(2,1)S(1)} %shard_map.76.refs_2_), channel_id=1, source_target_pairs={{0,12},{2,14},{1,13},{3,15},{4,8},{6,10},{5,9},{7,11},{8,4},{10,6}... | collective-permute-start | bytes 1277960 | tf_op jit(solution)/shard_map/ppermute | solution.py:28
  39.3 3.5 %collective-permute-start.11 = (bf16[128,1664]{1,0:T(8,128)(2,1)S(1)}, bf16[128,1664]{1,0:T(8,128)(2,1)S(1)}, u32[]{:S(2)}, u32[]{:S(2)}) collective-permute-start(bf16[128,1664]{1,0:T(8,128)(2,1)S(1)} %shard_map.78.refs_2_), channel_id=1, source_target_pairs={{0,3},{2,1},{1,2},{3,0},{4,7},{6,5},{5,6},{7,4},{8,11},{10,9},{9,1... | collective-permute-start | bytes 1277960 | tf_op jit(solution)/shard_map/ppermute | solution.py:28
  43.4 2.3 %collective-permute-done.5.refs_2_ = bf16[128,1664]{1,0:T(8,128)(2,1)S(1)} collective-permute-done((bf16[128,1664]{1,0:T(8,128)(2,1)S(1)}, bf16[128,1664]{1,0:T(8,128)(2,1)S(1)}, u32[]{:S(2)}, u32[]{:S(2)}) %collective-permute-start.5) | collective-permute-done | bytes 426016 | tf_op jit(solution)/shard_map/ppermute | solution.py:28
  45.9 2.0 %collective-permute-start.9 = (bf16[128,1664]{1,0:T(8,128)(2,1)S(1)}, bf16[128,1664]{1,0:T(8,128)(2,1)S(1)}, u32[]{:S(2)}, u32[]{:S(2)}) collective-permute-start(bf16[128,1664]{1,0:T(8,128)(2,1)S(1)} %get-tuple-element.30), channel_id=1, source_target_pairs={{0,2},{2,0},{1,3},{3,1},{4,6},{6,4},{5,7},{7,5},{8,10},{10,8},{9,1... | collective-permute-start | bytes 1277960 | tf_op jit(solution)/shard_map/ppermute | solution.py:28
  48.1 3.5 %collective-permute-start.16 = (bf16[128,1664]{1,0:T(8,128)(2,1)S(1)}, bf16[128,1664]{1,0:T(8,128)(2,1)S(1)}, u32[]{:S(2)}, u32[]{:S(2)}) collective-permute-start(bf16[128,1664]{1,0:T(8,128)(2,1)S(1)} %get-tuple-element.38), channel_id=1, source_target_pairs={{0,3},{2,1},{1,2},{3,0},{4,7},{6,5},{5,6},{7,4},{8,11},{10,9},{9,1... | collective-permute-start | bytes 1277960 | tf_op jit(solution)/shard_map/ppermute | solution.py:28
  54.2 2.8 %collective-permute-done.9.refs_1_ = bf16[128,1664]{1,0:T(8,128)(2,1)S(1)} collective-permute-done((bf16[128,1664]{1,0:T(8,128)(2,1)S(1)}, bf16[128,1664]{1,0:T(8,128)(2,1)S(1)}, u32[]{:S(2)}, u32[]{:S(2)}) %collective-permute-start.9) | collective-permute-done | bytes 426016 | tf_op jit(solution)/shard_map/ppermute | solution.py:28
  57.1 3.5 %collective-permute-start.13 = (bf16[128,1664]{1,0:T(8,128)(2,1)S(1)}, bf16[128,1664]{1,0:T(8,128)(2,1)S(1)}, u32[]{:S(2)}, u32[]{:S(2)}) collective-permute-start(bf16[128,1664]{1,0:T(8,128)(2,1)S(1)} %get-tuple-element.35), channel_id=1, source_target_pairs={{0,3},{2,1},{1,2},{3,0},{4,7},{6,5},{5,6},{7,4},{8,11},{10,9},{9,1... | collective-permute-start | bytes 1277960 | tf_op jit(solution)/shard_map/ppermute | solution.py:28
  63.5 5.9 %collective-permute-done.13.refs_1_ = bf16[128,1664]{1,0:T(8,128)(2,1)S(1)} collective-permute-done((bf16[128,1664]{1,0:T(8,128)(2,1)S(1)}, bf16[128,1664]{1,0:T(8,128)(2,1)S(1)}, u32[]{:S(2)}, u32[]{:S(2)}) %collective-permute-start.13) | collective-permute-done | bytes 426016 | tf_op jit(solution)/shard_map/ppermute | solution.py:28
  74.3 2.0 %collective-permute-start.24 = (bf16[128,1664]{1,0:T(8,128)(2,1)S(1)}, bf16[128,1664]{1,0:T(8,128)(2,1)S(1)}, u32[]{:S(2)}, u32[]{:S(2)}) collective-permute-start(bf16[128,1664]{1,0:T(8,128)(2,1)S(1)} %shard_map.92.refs_1_), channel_id=1, source_target_pairs={{0,12},{2,14},{1,13},{3,15},{4,8},{6,10},{5,9},{7,11},{8,4},{10,6}... | collective-permute-start | bytes 1277960 | tf_op jit(solution)/shard_map/ppermute | solution.py:28
  76.3 6.6 %collective-permute-done.17.refs_2_.refs_1_.refs_0_ = bf16[128,1664]{1,0:T(8,128)(2,1)S(1)} collective-permute-done((bf16[128,1664]{1,0:T(8,128)(2,1)S(1)}, bf16[128,1664]{1,0:T(8,128)(2,1)S(1)}, u32[]{:S(2)}, u32[]{:S(2)}) %collective-permute-start.17) | collective-permute-done | bytes 426016 | tf_op jit(solution)/shard_map/ppermute | solution.py:28
  86.2 2.1 %shard_map.97.refs_1_.refs_0_ = f32[256,928]{1,0:T(8,128)S(1)} custom-call(bf16[128,1664]{1,0:T(8,128)(2,1)S(1)} %shard_map.88.refs_2_.refs_0_, bf16[128,1664]{1,0:T(8,128)(2,1)S(1)} %collective-permute-done.17.refs_2_.refs_1_.refs_0_, bf16[128,1664]{1,0:T(8,128)(2,1)S(1)} %shard_map.89.refs_2_.refs_0_, ...), custom_call_target="tpu_custom_call" | custom-call | flops 1581252608 | bytes 14057472 | tf_op jit(solution)/shard_map/pallas_call | solution.py:61
  88.3 3.8 %collective-permute-done.24.refs_2_.refs_1_ = bf16[128,1664]{1,0:T(8,128)(2,1)S(1)} collective-permute-done((bf16[128,1664]{1,0:T(8,128)(2,1)S(1)}, bf16[128,1664]{1,0:T(8,128)(2,1)S(1)}, u32[]{:S(2)}, u32[]{:S(2)}) %collective-permute-start.24) | collective-permute-done | bytes 426016 | tf_op jit(solution)/shard_map/ppermute | solution.py:28
  94.8 2.1 %shard_map.101.refs_4_.refs_0_ = f32[256,928]{1,0:T(8,128)S(1)} custom-call(bf16[128,1664]{1,0:T(8,128)(2,1)S(1)} %shard_map.90.refs_2_.refs_0_, bf16[128,1664]{1,0:T(8,128)(2,1)S(1)} %collective-permute-done.22.refs_2_.refs_0_.refs_1_, bf16[128,1664]{1,0:T(8,128)(2,1)S(1)} %shard_map.91.refs_1_.refs_2_.refs_0_, ...), custom_call_target="tpu_custom_call" | custom-call | flops 1581252608 | bytes 14057472 | tf_op jit(solution)/shard_map/pallas_call | solution.py:61
  96.9 4.3 %collective-permute-done.25.refs_2_ = bf16[128,1664]{1,0:T(8,128)(2,1)S(1)} collective-permute-done((bf16[128,1664]{1,0:T(8,128)(2,1)S(1)}, bf16[128,1664]{1,0:T(8,128)(2,1)S(1)}, u32[]{:S(2)}, u32[]{:S(2)}) %collective-permute-start.25) | collective-permute-done | bytes 426016 | tf_op jit(solution)/shard_map/ppermute | solution.py:28
  106.5 2.6 %collective-permute-start.32 = (bf16[256,928]{1,0:T(8,128)(2,1)S(1)}, bf16[256,928]{1,0:T(8,128)(2,1)S(1)}, u32[]{:S(2)}, u32[]{:S(2)}) collective-permute-start(bf16[256,928]{1,0:T(8,128)(2,1)S(1)} %shard_map.107.refs_2_), channel_id=1, source_target_pairs={{0,16},{16,0},{32,48},{48,32},{64,80},{80,64},{96,112},{112,96},{1... | collective-permute-start | bytes 1425416 | tf_op jit(solution)/shard_map/ppermute | solution.py:37
  110.7 2.1 %collective-permute-start.33 = (bf16[64,928]{1,0:T(8,128)(2,1)S(1)}, bf16[64,928]{1,0:T(8,128)(2,1)S(1)}, u32[]{:S(2)}, u32[]{:S(2)}) collective-permute-start(bf16[64,928]{1,0:T(8,128)(2,1)S(1)} %get-tuple-element.46), channel_id=1, source_target_pairs={{64,0},{80,16},{96,32},{112,48},{0,64},{16,80},{32,96},{48,112},{6... | collective-permute-start | bytes 356360 | tf_op jit(solution)/shard_map/ppermute | solution.py:33
  114.3 2.8 %collective-permute-done.33.refs_1_ = bf16[64,928]{1,0:T(8,128)(2,1)S(1)} collective-permute-done((bf16[64,928]{1,0:T(8,128)(2,1)S(1)}, bf16[64,928]{1,0:T(8,128)(2,1)S(1)}, u32[]{:S(2)}, u32[]{:S(2)}) %collective-permute-start.33) | collective-permute-done | bytes 118816 | tf_op jit(solution)/shard_map/ppermute | solution.py:33
  117.0 2.1 %collective-permute-done.34.refs_2_ = bf16[64,928]{1,0:T(8,128)(2,1)S(1)} collective-permute-done((bf16[64,928]{1,0:T(8,128)(2,1)S(1)}, bf16[64,928]{1,0:T(8,128)(2,1)S(1)}, u32[]{:S(2)}, u32[]{:S(2)}) %collective-permute-start.34) | collective-permute-done | bytes 118816 | tf_op jit(solution)/shard_map/ppermute | solution.py:33
  (102 shorter events, 44.3 us)
Async XLA Ops:
  13.3 20.6 %collective-permute-start.4 = (bf16[256,1664]{1,0:T(8,128)(2,1)S(1)}, bf16[256,1664]{1,0:T(8,128)(2,1)S(1)}, u32[]{:S(2)}, u32[]{:S(2)}) collective-permute-start(bf16[256,1664]{1,0:T(8,128)(2,1)S(1)} %shard_map.66.refs_2_), channel_id=1, source_target_pairs={{0,4},{2,6},{1,5},{3,7},{4,0},{6,2},{5,1},{7,3},{8,12},{10,14},{9,... | collective-permute-start | bytes 2555912 | tf_op jit(solution)/shard_map/ppermute | solution.py:28
  15.8 21.5 %collective-permute-start.8 = (bf16[256,1664]{1,0:T(8,128)(2,1)S(1)}, bf16[256,1664]{1,0:T(8,128)(2,1)S(1)}, u32[]{:S(2)}, u32[]{:S(2)}) collective-permute-start(bf16[256,1664]{1,0:T(8,128)(2,1)S(1)} %shard_map.67.refs_2_), channel_id=1, source_target_pairs={{0,12},{2,14},{1,13},{3,15},{4,8},{6,10},{5,9},{7,11},{8,4},{10,6}... | collective-permute-start | bytes 2555912 | tf_op jit(solution)/shard_map/ppermute | solution.py:28
  18.9 20.4 %collective-permute-start.7 = (bf16[256,1664]{1,0:T(8,128)(2,1)S(1)}, bf16[256,1664]{1,0:T(8,128)(2,1)S(1)}, u32[]{:S(2)}, u32[]{:S(2)}) collective-permute-start(bf16[256,1664]{1,0:T(8,128)(2,1)S(1)} %shard_map.68.refs_2_), channel_id=1, source_target_pairs={{0,2},{2,0},{1,3},{3,1},{4,6},{6,4},{5,7},{7,5},{8,10},{10,8},{9,1... | collective-permute-start | bytes 2555912 | tf_op jit(solution)/shard_map/ppermute | solution.py:28
  21.8 21.1 %collective-permute-start.6 = (bf16[256,1664]{1,0:T(8,128)(2,1)S(1)}, bf16[256,1664]{1,0:T(8,128)(2,1)S(1)}, u32[]{:S(2)}, u32[]{:S(2)}) collective-permute-start(bf16[256,1664]{1,0:T(8,128)(2,1)S(1)} %shard_map.69.refs_2_), channel_id=1, source_target_pairs={{0,3},{2,1},{1,2},{3,0},{4,7},{6,5},{5,6},{7,4},{8,11},{10,9},{9,1... | collective-permute-start | bytes 2555912 | tf_op jit(solution)/shard_map/ppermute | solution.py:28
  34.0 11.7 %collective-permute-start.5 = (bf16[128,1664]{1,0:T(8,128)(2,1)S(1)}, bf16[128,1664]{1,0:T(8,128)(2,1)S(1)}, u32[]{:S(2)}, u32[]{:S(2)}) collective-permute-start(bf16[128,1664]{1,0:T(8,128)(2,1)S(1)} %shard_map.76.refs_2_), channel_id=1, source_target_pairs={{0,12},{2,14},{1,13},{3,15},{4,8},{6,10},{5,9},{7,11},{8,4},{10,6}... | collective-permute-start | bytes 1277960 | tf_op jit(solution)/shard_map/ppermute | solution.py:28
  37.4 10.5 %collective-permute-start.12 = (bf16[128,1664]{1,0:T(8,128)(2,1)S(1)}, bf16[128,1664]{1,0:T(8,128)(2,1)S(1)}, u32[]{:S(2)}, u32[]{:S(2)}) collective-permute-start(bf16[128,1664]{1,0:T(8,128)(2,1)S(1)} %shard_map.77.refs_2_), channel_id=1, source_target_pairs={{0,2},{2,0},{1,3},{3,1},{4,6},{6,4},{5,7},{7,5},{8,10},{10,8},{9,1... | collective-permute-start | bytes 1277960 | tf_op jit(solution)/shard_map/ppermute | solution.py:28
  39.3 12.3 %collective-permute-start.11 = (bf16[128,1664]{1,0:T(8,128)(2,1)S(1)}, bf16[128,1664]{1,0:T(8,128)(2,1)S(1)}, u32[]{:S(2)}, u32[]{:S(2)}) collective-permute-start(bf16[128,1664]{1,0:T(8,128)(2,1)S(1)} %shard_map.78.refs_2_), channel_id=1, source_target_pairs={{0,3},{2,1},{1,2},{3,0},{4,7},{6,5},{5,6},{7,4},{8,11},{10,9},{9,1... | collective-permute-start | bytes 1277960 | tf_op jit(solution)/shard_map/ppermute | solution.py:28
  45.9 11.2 %collective-permute-start.9 = (bf16[128,1664]{1,0:T(8,128)(2,1)S(1)}, bf16[128,1664]{1,0:T(8,128)(2,1)S(1)}, u32[]{:S(2)}, u32[]{:S(2)}) collective-permute-start(bf16[128,1664]{1,0:T(8,128)(2,1)S(1)} %get-tuple-element.30), channel_id=1, source_target_pairs={{0,2},{2,0},{1,3},{3,1},{4,6},{6,4},{5,7},{7,5},{8,10},{10,8},{9,1... | collective-permute-start | bytes 1277960 | tf_op jit(solution)/shard_map/ppermute | solution.py:28
  48.1 12.5 %collective-permute-start.16 = (bf16[128,1664]{1,0:T(8,128)(2,1)S(1)}, bf16[128,1664]{1,0:T(8,128)(2,1)S(1)}, u32[]{:S(2)}, u32[]{:S(2)}) collective-permute-start(bf16[128,1664]{1,0:T(8,128)(2,1)S(1)} %get-tuple-element.38), channel_id=1, source_target_pairs={{0,3},{2,1},{1,2},{3,0},{4,7},{6,5},{5,6},{7,4},{8,11},{10,9},{9,1... | collective-permute-start | bytes 1277960 | tf_op jit(solution)/shard_map/ppermute | solution.py:28
  53.0 10.2 %collective-permute-start.14 = (bf16[128,1664]{1,0:T(8,128)(2,1)S(1)}, bf16[128,1664]{1,0:T(8,128)(2,1)S(1)}, u32[]{:S(2)}, u32[]{:S(2)}) collective-permute-start(bf16[128,1664]{1,0:T(8,128)(2,1)S(1)} %get-tuple-element.36), channel_id=1, source_target_pairs={{0,12},{2,14},{1,13},{3,15},{4,8},{6,10},{5,9},{7,11},{8,4},{10,6}... | collective-permute-start | bytes 1277960 | tf_op jit(solution)/shard_map/ppermute | solution.py:28
  57.1 12.3 %collective-permute-start.13 = (bf16[128,1664]{1,0:T(8,128)(2,1)S(1)}, bf16[128,1664]{1,0:T(8,128)(2,1)S(1)}, u32[]{:S(2)}, u32[]{:S(2)}) collective-permute-start(bf16[128,1664]{1,0:T(8,128)(2,1)S(1)} %get-tuple-element.35), channel_id=1, source_target_pairs={{0,3},{2,1},{1,2},{3,0},{4,7},{6,5},{5,6},{7,4},{8,11},{10,9},{9,1... | collective-permute-start | bytes 1277960 | tf_op jit(solution)/shard_map/ppermute | solution.py:28
  60.7 10.0 %collective-permute-start.18 = (bf16[128,1664]{1,0:T(8,128)(2,1)S(1)}, bf16[128,1664]{1,0:T(8,128)(2,1)S(1)}, u32[]{:S(2)}, u32[]{:S(2)}) collective-permute-start(bf16[128,1664]{1,0:T(8,128)(2,1)S(1)} %get-tuple-element.42), channel_id=1, source_target_pairs={{0,4},{2,6},{1,5},{3,7},{4,0},{6,2},{5,1},{7,3},{8,12},{10,14},{9,... | collective-permute-start | bytes 1277960 | tf_op jit(solution)/shard_map/ppermute | solution.py:28
  61.3 10.7 %collective-permute-start.21 = (bf16[128,1664]{1,0:T(8,128)(2,1)S(1)}, bf16[128,1664]{1,0:T(8,128)(2,1)S(1)}, u32[]{:S(2)}, u32[]{:S(2)}) collective-permute-start(bf16[128,1664]{1,0:T(8,128)(2,1)S(1)} %get-tuple-element.44), channel_id=1, source_target_pairs={{0,12},{2,14},{1,13},{3,15},{4,8},{6,10},{5,9},{7,11},{8,4},{10,6}... | collective-permute-start | bytes 1277960 | tf_op jit(solution)/shard_map/ppermute | solution.py:28
  63.3 10.6 %collective-permute-start.20 = (bf16[128,1664]{1,0:T(8,128)(2,1)S(1)}, bf16[128,1664]{1,0:T(8,128)(2,1)S(1)}, u32[]{:S(2)}, u32[]{:S(2)}) collective-permute-start(bf16[128,1664]{1,0:T(8,128)(2,1)S(1)} %get-tuple-element.43), channel_id=1, source_target_pairs={{0,2},{2,0},{1,3},{3,1},{4,6},{6,4},{5,7},{7,5},{8,10},{10,8},{9,1... | collective-permute-start | bytes 1277960 | tf_op jit(solution)/shard_map/ppermute | solution.py:28
  69.7 13.2 %collective-permute-start.17 = (bf16[128,1664]{1,0:T(8,128)(2,1)S(1)}, bf16[128,1664]{1,0:T(8,128)(2,1)S(1)}, u32[]{:S(2)}, u32[]{:S(2)}) collective-permute-start(bf16[128,1664]{1,0:T(8,128)(2,1)S(1)} %shard_map.88.refs_2_.refs_0_), channel_id=1, source_target_pairs={{0,12},{2,14},{1,13},{3,15},{4,8},{6,10},{5,9},{7,11},{8,4},{10,6}... | collective-permute-start | bytes 1277960 | tf_op jit(solution)/shard_map/ppermute | solution.py:28
  71.0 12.3 %collective-permute-start.19 = (bf16[128,1664]{1,0:T(8,128)(2,1)S(1)}, bf16[128,1664]{1,0:T(8,128)(2,1)S(1)}, u32[]{:S(2)}, u32[]{:S(2)}) collective-permute-start(bf16[128,1664]{1,0:T(8,128)(2,1)S(1)} %shard_map.89.refs_2_.refs_0_), channel_id=1, source_target_pairs={{0,2},{2,0},{1,3},{3,1},{4,6},{6,4},{5,7},{7,5},{8,10},{10,8},{9,1... | collective-permute-start | bytes 1277960 | tf_op jit(solution)/shard_map/ppermute | solution.py:28
  72.2 13.0 %collective-permute-start.22 = (bf16[128,1664]{1,0:T(8,128)(2,1)S(1)}, bf16[128,1664]{1,0:T(8,128)(2,1)S(1)}, u32[]{:S(2)}, u32[]{:S(2)}) collective-permute-start(bf16[128,1664]{1,0:T(8,128)(2,1)S(1)} %shard_map.90.refs_2_.refs_0_), channel_id=1, source_target_pairs={{0,3},{2,1},{1,2},{3,0},{4,7},{6,5},{5,6},{7,4},{8,11},{10,9},{9,1... | collective-permute-start | bytes 1277960 | tf_op jit(solution)/shard_map/ppermute | solution.py:28
  74.1 11.3 %collective-permute-start.23 = (bf16[128,1664]{1,0:T(8,128)(2,1)S(1)}, bf16[128,1664]{1,0:T(8,128)(2,1)S(1)}, u32[]{:S(2)}, u32[]{:S(2)}) collective-permute-start(bf16[128,1664]{1,0:T(8,128)(2,1)S(1)} %shard_map.91.refs_1_.refs_2_.refs_0_), channel_id=1, source_target_pairs={{0,4},{2,6},{1,5},{3,7},{4,0},{6,2},{5,1},{7,3},{8,12},{10,14},{9,... | collective-permute-start | bytes 1277960 | tf_op jit(solution)/shard_map/ppermute | solution.py:28
  74.3 17.8 %collective-permute-start.24 = (bf16[128,1664]{1,0:T(8,128)(2,1)S(1)}, bf16[128,1664]{1,0:T(8,128)(2,1)S(1)}, u32[]{:S(2)}, u32[]{:S(2)}) collective-permute-start(bf16[128,1664]{1,0:T(8,128)(2,1)S(1)} %shard_map.92.refs_1_), channel_id=1, source_target_pairs={{0,12},{2,14},{1,13},{3,15},{4,8},{6,10},{5,9},{7,11},{8,4},{10,6}... | collective-permute-start | bytes 1277960 | tf_op jit(solution)/shard_map/ppermute | solution.py:28
  83.4 10.9 %collective-permute-start.27 = (bf16[128,1664]{1,0:T(8,128)(2,1)S(1)}, bf16[128,1664]{1,0:T(8,128)(2,1)S(1)}, u32[]{:S(2)}, u32[]{:S(2)}) collective-permute-start(bf16[128,1664]{1,0:T(8,128)(2,1)S(1)} %shard_map.94.refs_1_), channel_id=1, source_target_pairs={{0,3},{2,1},{1,2},{3,0},{4,7},{6,5},{5,6},{7,4},{8,11},{10,9},{9,1... | collective-permute-start | bytes 1277960 | tf_op jit(solution)/shard_map/ppermute | solution.py:28
  85.5 15.7 %collective-permute-start.25 = (bf16[128,1664]{1,0:T(8,128)(2,1)S(1)}, bf16[128,1664]{1,0:T(8,128)(2,1)S(1)}, u32[]{:S(2)}, u32[]{:S(2)}) collective-permute-start(bf16[128,1664]{1,0:T(8,128)(2,1)S(1)} %shard_map.96.refs_5_), channel_id=1, source_target_pairs={{0,12},{2,14},{1,13},{3,15},{4,8},{6,10},{5,9},{7,11},{8,4},{10,6}... | collective-permute-start | bytes 1277960 | tf_op jit(solution)/shard_map/ppermute | solution.py:28
  92.1 10.3 %collective-permute-start.30 = (bf16[128,1664]{1,0:T(8,128)(2,1)S(1)}, bf16[128,1664]{1,0:T(8,128)(2,1)S(1)}, u32[]{:S(2)}, u32[]{:S(2)}) collective-permute-start(bf16[128,1664]{1,0:T(8,128)(2,1)S(1)} %shard_map.98.refs_1_), channel_id=1, source_target_pairs={{0,2},{2,0},{1,3},{3,1},{4,6},{6,4},{5,7},{7,5},{8,10},{10,8},{9,1... | collective-permute-start | bytes 1277960 | tf_op jit(solution)/shard_map/ppermute | solution.py:28
  92.5 11.0 %collective-permute-start.31 = (bf16[128,1664]{1,0:T(8,128)(2,1)S(1)}, bf16[128,1664]{1,0:T(8,128)(2,1)S(1)}, u32[]{:S(2)}, u32[]{:S(2)}) collective-permute-start(bf16[128,1664]{1,0:T(8,128)(2,1)S(1)} %shard_map.99.refs_1_), channel_id=1, source_target_pairs={{0,3},{2,1},{1,2},{3,0},{4,7},{6,5},{5,6},{7,4},{8,11},{10,9},{9,1... | collective-permute-start | bytes 1277960 | tf_op jit(solution)/shard_map/ppermute | solution.py:28
  94.4 10.6 %collective-permute-start.29 = (bf16[128,1664]{1,0:T(8,128)(2,1)S(1)}, bf16[128,1664]{1,0:T(8,128)(2,1)S(1)}, u32[]{:S(2)}, u32[]{:S(2)}) collective-permute-start(bf16[128,1664]{1,0:T(8,128)(2,1)S(1)} %shard_map.100.refs_5_), channel_id=1, source_target_pairs={{0,4},{2,6},{1,5},{3,7},{4,0},{6,2},{5,1},{7,3},{8,12},{10,14},{9,... | collective-permute-start | bytes 1277960 | tf_op jit(solution)/shard_map/ppermute | solution.py:28
  (15 other events, 104.9 us)
